TPU v7x, 256 devices: a whole 4x4x8 slice. The times are simulated.
256 devices in a mesh: seq: 32 (over y_lo, z, core), exp: 8 (over y_hi, x).
Axes of the slice: x: 4, y: 4 (y_hi: 2, y_lo: 2; y = y_hi * 2 + y_lo), z: 8, core: 2. Of those that a mesh axis runs over, the one named last changes fastest.
Arguments:
- tokens: bfloat16 [3, 65536, 1280], P(None, ('seq', 'exp')), may hold values from -64 to 64
- router: bfloat16 [1280, 128], replicated, may hold values from -1 to 1
- w_in: bfloat16 [64, 1280, 5120], P('seq', None, 'exp'), may hold values from -0.15625 to 0.15625
- w_out: bfloat16 [64, 5120, 1280], P('seq', 'exp'), may hold values from -0.078125 to 0.078125
- cotangent: bfloat16 [3, 65536, 1280], P(None, ('seq', 'exp')), may hold values from -6 to 6
Outputs:
- d_tokens: bfloat16 [3, 65536, 1280], P(None, ('seq', 'exp'))
- d_router: float32 [1280, 128], replicated
All inputs are finite; a program needn't handle non-finite values.
Results may differ from a plain program's by a relative error of at most 0.02.
Values may be sent and summed in bfloat16 or wider, within the bound.
No kernel may reach another device: no remote copies, remote signals or barrier semaphores. Data moves between devices by JAX's collectives and lax.ppermute only.
A program may use at most 64 MiB of HBM per device.

v0:
```python
import jax
import jax.numpy as jnp
from jax import lax
from jax.sharding import PartitionSpec as P

SPE = 2


def gelu_tanh(values):
    return jax.nn.gelu(values, approximate=True)


def to_owners(stacked):
    summed = lax.psum(stacked, ("seq", "exp"))
    per_owner = stacked.shape[2] // lax.axis_size("seq")
    return lax.dynamic_slice_in_dim(summed, lax.axis_index("seq") * per_owner, per_owner, 2)


def to_tokens(stacked):
    summed = lax.psum(stacked.astype(jnp.bfloat16), "exp")
    return lax.all_gather(summed, "seq", axis=2, tiled=True)


def expert_forward(slot_in, w_in, w_out):
    clips = slot_in.shape[0]
    grouped = slot_in.reshape(clips, w_in.shape[0], SPE, slot_in.shape[2])
    preact = jnp.einsum("cesd,edh->cesh", grouped, w_in, preferred_element_type=jnp.float32)
    hidden = gelu_tanh(preact).astype(jnp.bfloat16)
    part_out = jnp.einsum("cesh,ehd->cesd", hidden, w_out, preferred_element_type=jnp.float32)
    return (preact, part_out.reshape(clips, -1, slot_in.shape[2]))


def expert_backward(preact, d_slot_out, w_in, w_out):
    clips = d_slot_out.shape[0]
    grads = d_slot_out.reshape(clips, w_in.shape[0], SPE, d_slot_out.shape[2])
    d_hidden = jnp.einsum("cesd,ehd->cesh", grads, w_out, preferred_element_type=jnp.float32)
    d_preact = jax.vjp(gelu_tanh, preact)[1](d_hidden)[0].astype(jnp.bfloat16)
    part_din = jnp.einsum("cesh,edh->cesd", d_preact, w_in, preferred_element_type=jnp.float32)
    return part_din.reshape(clips, -1, d_slot_out.shape[2])


def per_device(tokens, router, w_in, w_out, cotangent):
    logits = jnp.einsum("cnd,ds->cns", tokens, router, preferred_element_type=jnp.float32)
    local_peak = jnp.max(logits, axis=1)
    col_peak = lax.pmax(local_peak, ("seq", "exp"))
    col_exp = jnp.exp(logits - col_peak[:, None, :])
    col_sum = lax.psum(jnp.sum(col_exp, axis=1), ("seq", "exp"))
    dispatch = col_exp / col_sum[:, None, :]
    dispatch_low = dispatch.astype(jnp.bfloat16)
    partial_in = jnp.einsum(
        "cns,cnd->csd", dispatch_low, tokens, preferred_element_type=jnp.float32
    )
    row_peak = jnp.max(logits, axis=2, keepdims=True)
    row_exp = jnp.exp(logits - row_peak)
    combine = row_exp / jnp.sum(row_exp, axis=2, keepdims=True)
    combine_low = combine.astype(jnp.bfloat16)
    slot_in = to_owners(partial_in[:, None]).astype(jnp.bfloat16)[:, 0]
    preact, part_out = expert_forward(slot_in, w_in, w_out)
    slot_out = to_tokens(part_out[:, None])[:, 0]
    partial_dout = jnp.einsum(
        "cns,cnd->csd", combine_low, cotangent, preferred_element_type=jnp.float32
    )
    d_slot_out = to_owners(partial_dout[:, None]).astype(jnp.bfloat16)[:, 0]
    d_combine = jnp.einsum("cnd,csd->cns", cotangent, slot_out, preferred_element_type=jnp.float32)
    d_logit_c = combine * (d_combine - jnp.sum(combine * d_combine, axis=2, keepdims=True))
    part_din = expert_backward(preact, d_slot_out, w_in, w_out)
    d_slot_in = to_tokens(part_din[:, None])[:, 0]
    d_via_slots = jnp.einsum(
        "cns,csd->cnd", dispatch_low, d_slot_in, preferred_element_type=jnp.float32
    )
    d_dispatch = jnp.einsum("cnd,csd->cns", tokens, d_slot_in, preferred_element_type=jnp.float32)
    column_dot = lax.psum(jnp.sum(dispatch * d_dispatch, axis=1), ("seq", "exp"))
    d_logit = (d_logit_c + dispatch * (d_dispatch - column_dot[:, None, :])).astype(jnp.bfloat16)
    d_tokens = (
        d_via_slots + jnp.einsum("cns,ds->cnd", d_logit, router, preferred_element_type=jnp.float32)
    ).astype(jnp.bfloat16)
    router_part = jnp.einsum("cnd,cns->ds", tokens, d_logit, preferred_element_type=jnp.float32)
    d_router = lax.psum(router_part, ("seq", "exp"))
    return (d_tokens, d_router)


def solution(mesh):
    placed = (
        P(None, ("seq", "exp"), None),
        P(),
        P("seq", None, "exp"),
        P("seq", "exp", None),
        P(None, ("seq", "exp"), None),
    )
    return jax.shard_map(
        per_device,
        mesh=mesh,
        in_specs=placed,
        out_specs=(P(None, ("seq", "exp"), None), P()),
        check_vma=False,
    )
```

profile of v0, /device:TPU:1, one launch (start us, length us, event | category | flops | bytes accessed | tf_op | source)
XLA Modules:
  0.0 766.9 jit_solution(17202288305853177197)
XLA Ops:
  7.2 0.0 copy-start
  7.2 0.0 all-reduce.5.cloned.1.call-start
  7.2 3.1 fusion.88
  10.4 81.4 %pmax.7 = f32[3,128]{1,0:T(4,128)S(1)} all-reduce(f32[3,128]{1,0:T(4,128)S(1)} %get-tuple-element.10), channel_id=1, replica_groups=mesh['seq'=32,'exp'=8] {'seq','exp'}, use_global_device_ids=true, to_apply=%region_1.0 | all-reduce | flops 384 | bytes 3072 | tf_op jit(solution)/shard_map/pmax | solution.py:45
  91.8 2.2 fusion.89
  93.9 1.1 fusion.41
  95.0 72.4 %psum.49 = f32[3,128]{1,0:T(4,128)S(1)} all-reduce(f32[3,128]{1,0:T(4,128)S(1)} %fusion.41), channel_id=1, replica_groups=mesh['seq'=32,'exp'=8] {'seq','exp'}, use_global_device_ids=true, to_apply=%region_3.0 | all-reduce | flops 384 | bytes 3072 | tf_op jit(solution)/shard_map/psum | solution.py:47
  167.4 3.4 convolution_bitcast_fusion
  170.8 4.7 convolution_bitcast_fusion.1
  175.6 128.6 %all-reduce.6 = (bf16[3,1,128,1280]{3,2,0,1:T(8,128)(2,1)}, bf16[3,1,128,1280]{3,2,0,1:T(8,128)(2,1)}) all-reduce(f32[3,1,128,1280]{3,2,0,1:T(8,128)} %convolution_bitcast_fusion, f32[3,1,128,1280]{3,2,0,1:T(8,128)} %convolution_bitcast_fusion.1), channel_id=1, replica_groups=mesh['seq'=32,'exp'=8] {'seq','exp'}, use_global_device_ids=true, to_apply=%region_7.0 | all-reduce | flops 983040 | bytes 5898240 | tf_op jit(solution)/shard_map/psum | solution.py:14
  304.2 0.9 dynamic-slice_convert_fusion
  305.2 2.5 fusion.26
  307.7 0.0 copy-done
  307.7 0.6 fusion.11
  308.3 3.8 fusion.14
  312.1 35.0 %all-reduce.1 = (bf16[3,1,4,1280]{3,0,1,2:T(4,128)(2,1)S(1)}, bf16[3,1,4,1280]{3,0,1,2:T(4,128)(2,1)S(1)}) all-reduce(bf16[3,1,4,1280]{3,0,1,2:T(4,128)(2,1)S(1)} %bitcast.87, bf16[3,1,4,1280]{3,0,1,2:T(4,128)(2,1)S(1)} %bitcast.85), channel_id=1, replica_groups=mesh['seq'=32,'exp'=8] {'exp'}, use_global_device_ids=true, to_apply=%region_9.0 | all-reduce | flops 30720 | bytes 122880 | tf_op jit(solution)/shard_map/psum | solution.py:20
  347.1 42.1 %all_gather.6 = bf16[3,1,128,1280]{3,0,1,2:T(4,128)(2,1)S(1)} all-gather(bf16[3,1,4,1280]{3,0,1,2:T(4,128)(2,1)S(1)} %get-tuple-element.9), channel_id=1, replica_groups=mesh['seq'=32,'exp'=8] {'seq'}, dimensions={2}, use_global_device_ids=true | all-gather | bytes 1013760 | tf_op jit(solution)/shard_map/all_gather | solution.py:21
  389.2 0.0 copy-start.1
  389.2 3.5 multiply_reduce_fusion.1
  392.7 0.0 copy-done.1
  392.7 73.9 %psum.54 = f32[3,128]{1,0:T(4,128)S(1)} all-reduce(f32[3,128]{1,0:T(4,128)S(1)} %get-tuple-element.14), channel_id=1, replica_groups=mesh['seq'=32,'exp'=8] {'seq','exp'}, use_global_device_ids=true, to_apply=%region_12.0 | all-reduce | flops 384 | bytes 3072 | tf_op jit(solution)/shard_map/psum | solution.py:72
  466.6 36.9 %all_gather.7 = bf16[3,1,128,1280]{3,0,1,2:T(4,128)(2,1)S(1)} all-gather(bf16[3,1,4,1280]{3,0,1,2:T(4,128)(2,1)S(1)} %get-tuple-element.8), channel_id=1, replica_groups=mesh['seq'=32,'exp'=8] {'seq'}, dimensions={2}, use_global_device_ids=true | all-gather | bytes 1013760 | tf_op jit(solution)/shard_map/all_gather | solution.py:21
  503.5 3.0 convolution_bitcast_fusion.4
  506.5 7.1 convolution_bitcast_fusion.2
  513.6 0.0 all-reduce.5.cloned.1.call-update
  513.6 7.2 fusion.29
  520.8 4.6 fusion.2
  525.4 232.5 %all-reduce.5.cloned.1.call-done = f32[1280,128]{0,1:T(8,128)} async-done(((f32[1280,128]{0,1:T(8,128)}), f32[1280,128]{0,1:T(8,128)}) %all-reduce.5.cloned.1.call-update) | async-done | bytes 655376 | tf_op jit(solution)/shard_map/psum | solution.py:78
  757.9 2.2 copy.28
  (2 shorter events, 0.0 us)
Async XLA Ops:
  7.2 300.5 %copy-start = (bf16[2,640,1280]{2,1,0:T(8,128)(2,1)S(1)}, bf16[2,640,1280]{2,1,0:T(8,128)(2,1)}, u32[]{:S(2)}) copy-start(bf16[2,640,1280]{2,1,0:T(8,128)(2,1)} %param.8) | copy-start | bytes 9830404
  7.2 750.7 %all-reduce.5.cloned.1.call-start = ((), (), s32[]{:S(2)}) async-start(), calls=%async_computation | async-start | bytes 1310720 | tf_op jit(solution)/shard_map/psum | solution.py:78
  389.2 3.5 copy-start.1
Sparse Core Ops, SparseCore 0:
  513.8 244.0 all-reduce.4
where the time goes:
time: 768 us; the launch traced here: 767 us
  blocking collectives  470 us (61%)
  waiting for transfers between devices  233 us (30%)
  matrix products  43.5 us (6%)
  between operations  14.1 us (2%)
    psum x1, waiting for transfers between devices, per_device(): d_router = lax.psum(router_part, ('seq', 'exp'))  232 us
    psum x1, blocking collectives, to_owners(): summed = lax.psum(stacked, ('seq', 'exp'))  129 us
    pmax x1, blocking collectives, per_device(): col_peak = lax.pmax(local_peak, ('seq', 'exp'))  81.4 us
    all_gather x2, blocking collectives, to_tokens(): return lax.all_gather(summed, 'seq', axis=2, tiled=True)  79 us
    psum x1, blocking collectives, per_device(): lax.psum(jnp.sum(dispatch * d_dispatch, axis=1), ('seq', 'exp'))  73.9 us
    psum x1, blocking collectives, per_device(): col_sum = lax.psum(jnp.sum(col_exp, axis=1), ('seq', 'exp'))  72.4 us
    psum x1, blocking collectives, to_tokens(): summed = lax.psum(stacked.astype(jnp.bfloat16), 'exp')  35 us
  transfers between devices with their start and end apart: 1, of which 1 were waited for; matrix products, arithmetic and copies ran while one was open for 2% of the time, Pallas kernels for 0%

commit v1 on v0

v1 whole, which is shorter than its diff:
```python
import functools

import jax
import jax.numpy as jnp
from jax import lax
from jax.experimental import pallas as pl
from jax.experimental.pallas import tpu as pltpu
from jax.sharding import Mesh, PartitionSpec as P

SIZES = {"yl": 2, "z": 8, "core": 2, "yh": 2, "x": 4}
AXES = tuple(SIZES)
OWNERS = ("yl", "z")
EXP = ("yh", "x")
PLANE = ("yl", "yh", "x")

D = 1280
WIDE = 1408
CLIPS = 3
TOK = 256
ROWS = 24
VMEM = 48 * 1024 * 1024
GELU_C = 0.7978845608028654
GELU_A = 0.044715

bf16 = jnp.bfloat16
f32 = jnp.float32

NT = (((1,), (1,)), ((), ()))
TN = (((0,), (0,)), ((), ()))


def dot(a, b, dims=None):
    if dims is None:
        return jnp.dot(a, b, preferred_element_type=f32)
    return lax.dot_general(a, b, dims, preferred_element_type=f32)


def is_grad_row(shape):
    return lax.broadcasted_iota(jnp.int32, shape, 0) % 8 >= 4


def swap_halves(v, grad):
    n = v.shape[0]
    return jnp.where(grad, pltpu.roll(v, 4, 0), pltpu.roll(v, n - 4, 0))


def pack_stats(columns):
    rows = columns[0].shape[0]
    lane = lax.broadcasted_iota(jnp.int32, (rows, 128), 1)
    out = jnp.zeros((rows, 128), f32)
    for i, value in enumerate(columns):
        high = value.astype(bf16).astype(f32)
        rest = value - high
        middle = rest.astype(bf16).astype(f32)
        for j, part in enumerate((high, middle, rest - middle)):
            out = jnp.where(lane == 3 * i + j, part, out)
    return out


def read_stat(stats, i):
    lane = lax.broadcasted_iota(jnp.int32, stats.shape, 1)
    kept = jnp.where((lane >= 3 * i) & (lane < 3 * i + 3), stats, 0.0)
    return jnp.sum(kept, axis=1, keepdims=True)


def merge(blocks):
    wide = [b.astype(f32) for b in blocks]
    peaks = [read_stat(b[:, D:], 0) for b in wide]
    sums = [read_stat(b[:, D:], 1) for b in wide]
    peak = functools.reduce(jnp.maximum, peaks)
    values = jnp.zeros((wide[0].shape[0], D), f32)
    total = jnp.zeros_like(peak)
    for b, p, s in zip(wide, peaks, sums):
        scale = jnp.exp(p - peak)
        values = values + scale * b[:, :D]
        total = total + scale * s
    return values, peak, total


def call(body, outs, *args, scratch=(), flops=0, nbytes=0, smem=()):
    specs = [
        pl.BlockSpec(memory_space=pltpu.SMEM if i in smem else pltpu.VMEM) for i in range(len(args))
    ]
    return pl.pallas_call(
        body,
        out_shape=[jax.ShapeDtypeStruct(s, t) for s, t in outs],
        in_specs=specs,
        out_specs=[pl.BlockSpec(memory_space=pltpu.VMEM) for _ in outs],
        scratch_shapes=list(scratch),
        compiler_params=pltpu.CompilerParams(vmem_limit_bytes=VMEM),
        cost_estimate=pl.CostEstimate(flops=flops, bytes_accessed=nbytes, transcendentals=0),
    )(*args)


def slots_body(core_ref, tokens, router, cot, mine, theirs, rt_ref, lt_ref, weights_in, weights_out):
    t = lax.broadcasted_iota(jnp.int32, (256, 128), 0)
    s = lax.broadcasted_iota(jnp.int32, (256, 128), 1)
    half = t // 128
    owner_core = half + core_ref[0] * (1 - 2 * half)
    slot = 8 * ((t % 128) // 8) + 4 * owner_core + t % 4
    pick = (s == slot).astype(f32).astype(bf16)
    rt_ref[...] = dot(pick, router[...], NT).astype(bf16)
    grad = is_grad_row((256, TOK))
    grad_col = is_grad_row((256, 1))
    stats = []
    for c in range(CLIPS):
        logits = dot(rt_ref[...], tokens[c], NT)
        lt_ref[c] = logits
        peak = jnp.max(logits, axis=1, keepdims=True)
        low = jnp.where(grad, 0.0, jnp.exp(logits - peak)).astype(bf16)
        total = jnp.sum(low.astype(f32), axis=1, keepdims=True)
        weights_in[c] = low
        raised = jnp.exp(logits - jnp.max(logits, axis=0, keepdims=True))
        combine = raised / (0.5 * jnp.sum(raised, axis=0, keepdims=True))
        weights_out[c] = jnp.where(grad, combine, 0.0).astype(bf16)
        peak = jnp.where(grad_col, 0.0, peak)
        total = jnp.where(grad_col, 1.0, total)
        stats.append(pack_stats([peak, total]).reshape(32, 8, 128))
    packed = jnp.concatenate(stats, axis=1).astype(bf16)
    mine[:, :, D:] = packed[:16]
    theirs[:, :, D:] = packed[16:]

    def chunk(j, carry):
        lanes = pl.ds(pl.multiple_of(j * 256, 256), 256)
        parts = []
        for c in range(CLIPS):
            part = dot(weights_in[c], tokens[c, :, lanes]) + dot(weights_out[c], cot[c, :, lanes])
            parts.append(part.reshape(32, 8, 256))
        full = jnp.concatenate(parts, axis=1).astype(bf16)
        mine[:, :, lanes] = full[:16]
        theirs[:, :, lanes] = full[16:]
        return carry

    lax.fori_loop(0, D // 256, chunk, 0)


def pair_body(a_ref, b_ref, out):
    for d in range(16):
        values, peak, total = merge([a_ref[d], b_ref[d]])
        out[d, :, :D] = values.astype(bf16)
        out[d, :, D:] = pack_stats([peak, total]).astype(bf16)


def owner_body(x_ref, out):
    values, peak, total = merge([x_ref[d] for d in range(16)])
    values = values.astype(bf16)
    stats = pack_stats([peak, total]).astype(bf16)
    for e in range(8):
        out[e, :, :D] = values
        out[e, :, D:] = stats


def gelu_parts(v):
    t = jnp.tanh(GELU_C * (v + GELU_A * (v * v * v)))
    value = 0.5 * v * (1.0 + t)
    slope = 0.5 * (1.0 + t) + 0.5 * v * (1.0 - t * t) * (GELU_C * (1.0 + 3.0 * GELU_A * (v * v)))
    return value, slope


def expert_body(x_ref, w_in, w_out, out, keep):
    values, peak, total = merge([x_ref[e] for e in range(8)])
    grad_col = is_grad_row((ROWS, 1))
    rows = values * jnp.where(grad_col, 1.0, 1.0 / total)
    keep[:, :D] = rows
    keep[:, D:] = pack_stats([peak, total])
    low = rows.astype(bf16)
    row = lax.broadcasted_iota(jnp.int32, (ROWS, 640), 0)
    grad = row % 8 >= 4
    acc = jnp.zeros((ROWS, D), f32)
    for i in range(2):
        own = (row % 4) // 2 == i
        value, slope = gelu_parts(dot(low, w_in[i]))
        d_pre = dot(low, w_out[i], NT) * pltpu.roll(slope, 4, 0)
        hidden = jnp.where(own & jnp.logical_not(grad), value, 0.0).astype(bf16)
        d_pre = jnp.where(own & grad, d_pre, 0.0).astype(bf16)
        acc = acc + dot(hidden, w_out[i]) + dot(d_pre, w_in[i], NT)
    acc = acc.astype(bf16)
    for e in range(8):
        out[e] = acc


def result_body(x_ref, keep, out):
    acc = x_ref[0].astype(f32)
    for e in range(1, 8):
        acc = acc + x_ref[e].astype(f32)
    low = acc.astype(bf16)
    slot_in = keep[:, :D]
    column_dot = jnp.sum(low.astype(f32) * pltpu.roll(slot_in, 4, 0), axis=1, keepdims=True)
    peak = read_stat(keep[:, D:], 0)
    total = read_stat(keep[:, D:], 1)
    grad = is_grad_row((ROWS, 128))
    own = jnp.where(
        grad,
        pack_stats([jnp.zeros_like(peak), jnp.zeros_like(peak), column_dot]),
        pack_stats([peak, total, jnp.zeros_like(peak)]),
    )
    stats = (own + swap_halves(own, grad)).astype(bf16)
    for d in range(16):
        out[d, :, :D] = low
        out[d, :, D:] = stats


def logit_body(tokens, cot, lt_ref, gm, gt, r_mine, r_theirs, dl_ref, w_ref, g_ref):
    grad = is_grad_row((256, TOK))
    g_mine = gm[...].astype(f32)
    g_theirs = gt[...].astype(f32)
    for c in range(CLIPS):
        rows = slice(8 * c, 8 * c + 8)
        both = jnp.concatenate(
            [g_mine[:, rows].reshape(128, WIDE), g_theirs[:, rows].reshape(128, WIDE)], axis=0
        )
        stats = both[:, D:]
        low = both[:, :D].astype(bf16)
        g_ref[c] = low
        peak, total, column_dot = (read_stat(stats, i) for i in range(3))
        logits = lt_ref[c]
        raised = jnp.exp(logits - jnp.max(logits, axis=0, keepdims=True))
        combine = raised / (0.5 * jnp.sum(raised, axis=0, keepdims=True))
        combine = jnp.where(grad, 0.0, combine)
        d_combine = dot(low, cot[c], NT)
        inner = jnp.sum(combine * d_combine, axis=0, keepdims=True)
        dispatch = jnp.where(grad, jnp.exp(logits - peak) * (1.0 / total), 0.0)
        d_dispatch = dot(low, tokens[c], NT)
        own = jnp.where(grad, dispatch * (d_dispatch - column_dot), combine * (d_combine - inner))
        d_logit = (own + swap_halves(own, grad)).astype(bf16)
        part = dot(d_logit, tokens[c])
        grad_half = is_grad_row((256, 640))
        part = jnp.where(grad_half, part[:, 640:], part[:, :640]).reshape(32, 8, 640)
        if c == 0:
            r_mine[...] = part[:16]
            r_theirs[...] = part[16:]
        else:
            r_mine[...] += part[:16]
            r_theirs[...] += part[16:]
        dl_ref[c] = jnp.where(grad, 0.0, d_logit.astype(f32)).astype(bf16)
        w_ref[c] = dispatch.astype(bf16)


def tokens_body(dl_ref, w_ref, rt_ref, g_ref, out):
    for c in range(CLIPS):
        out[c] = (dot(dl_ref[c], rt_ref[...], TN) + dot(w_ref[c], g_ref[c], TN)).astype(bf16)


def add_body(a_ref, b_ref, out):
    out[...] = a_ref[...] + b_ref[...]


def spread_body(x_ref, out):
    acc = x_ref[0]
    for i in range(1, x_ref.shape[0]):
        acc = acc + x_ref[i]
    for i in range(out.shape[0]):
        out[i] = acc


def router_body(core_ref, mine, theirs, out):
    t = lax.broadcasted_iota(jnp.int32, (256, 128), 0)
    s = lax.broadcasted_iota(jnp.int32, (256, 128), 1)
    half = t // 128
    owner_core = half + core_ref[0] * (1 - 2 * half)
    slot = 8 * ((t % 128) // 8) + 4 * owner_core + t % 4
    rows = jnp.concatenate([mine[...].reshape(128, 640), theirs[...].reshape(128, 640)], axis=0)
    high = rows.astype(bf16)
    rest = rows - high.astype(f32)
    middle = rest.astype(bf16)
    low = (rest - middle.astype(f32)).astype(bf16)
    for a in range(2):
        pick = ((s == slot) & ((t % 8) // 4 == a)).astype(f32).astype(bf16)
        moved = dot(high, pick, TN) + (dot(middle, pick, TN) + dot(low, pick, TN))
        out[a * 640 : (a + 1) * 640, :] = moved


def exchange(x, axes):
    return lax.all_to_all(x, axes, 0, 0, tiled=True)


def to_partner(x):
    return lax.ppermute(x, "core", [(0, 1), (1, 0)])


def per_device(tokens, router, w_in, w_out, cotangent):
    core = lax.axis_index("core").astype(jnp.int32).reshape(1)
    block = ((16, ROWS, WIDE), bf16)
    mine, theirs, rt, lt = call(
        slots_body,
        [block, block, ((256, D), bf16), ((CLIPS, 256, TOK), f32)],
        core,
        tokens,
        router,
        cotangent,
        scratch=[pltpu.VMEM((CLIPS, 256, TOK), bf16), pltpu.VMEM((CLIPS, 256, TOK), bf16)],
        smem=(0,),
        flops=3 * 10**9,
        nbytes=8 * 10**6,
    )
    (summed,) = call(pair_body, [block], mine, to_partner(theirs), nbytes=3 * 10**6)
    owned = exchange(summed, OWNERS)
    (owned,) = call(owner_body, [((8, ROWS, WIDE), bf16)], owned, nbytes=2 * 10**6)
    shared = exchange(owned, EXP)
    parts, keep = call(
        expert_body,
        [((8, ROWS, D), bf16), ((ROWS, WIDE), f32)],
        shared,
        w_in,
        w_out,
        flops=10**9,
        nbytes=8 * 10**6,
    )
    parts = exchange(parts, EXP)
    (result,) = call(result_body, [block], parts, keep, nbytes=2 * 10**6)
    g_mine = exchange(result, OWNERS)
    g_theirs = to_partner(g_mine)
    half = ((16, 8, 640), f32)
    square = ((CLIPS, 256, TOK), bf16)
    r_mine, r_theirs, d_logit, dispatch, grads = call(
        logit_body,
        [half, half, square, square, ((CLIPS, 256, D), bf16)],
        tokens,
        cotangent,
        lt,
        g_mine,
        g_theirs,
        flops=3 * 10**9,
        nbytes=10**7,
    )
    (r_mine,) = call(add_body, [half], r_mine, to_partner(r_theirs), nbytes=10**6)
    (d_tokens,) = call(
        tokens_body,
        [((CLIPS, TOK, D), bf16)],
        d_logit,
        dispatch,
        rt,
        grads,
        flops=10**9,
        nbytes=6 * 10**6,
    )
    r_mine = exchange(r_mine, PLANE)
    (r_mine,) = call(spread_body, [((8, 8, 640), f32)], r_mine, nbytes=10**6)
    r_mine = exchange(r_mine, ("z",))
    (r_mine,) = call(spread_body, [half], r_mine, nbytes=10**6)
    r_mine = exchange(r_mine, PLANE)
    (d_router,) = call(
        router_body, [((D, 128), f32)], core, r_mine, to_partner(r_mine), smem=(0,), nbytes=2 * 10**6
    )
    return (d_tokens, d_router)


def solution(mesh):
    fine = Mesh(mesh.devices.reshape(tuple(SIZES.values())), AXES)
    seq = ("yl", "z", "core")
    placed = (
        P(None, AXES, None),
        P(),
        P(seq, None, EXP),
        P(seq, EXP, None),
        P(None, AXES, None),
    )
    return jax.shard_map(
        per_device,
        mesh=fine,
        in_specs=placed,
        out_specs=(P(None, AXES, None), P()),
        check_vma=False,
    )
```

time: 768 us -> 169 us (0.22)
  blocking collectives: 470 us -> 126 us
  waiting for transfers between devices: 233 us -> 5.93 us
  matrix products: 43.5 us -> 0 us
  Pallas kernels: 0 us -> 20.6 us
  between operations: 14.1 us -> 0.7 us
  starting transfers between devices: 0.04 us -> 13.1 us
    psum x4 -> x0, blocking collectives: 310 us -> none  [the longest x1 129 us: to_owners(): summed = lax.psum(stacked, ('seq', 'exp'))]
    psum x1 -> x0, waiting for transfers between devices: 232 us -> none  [per_device(): d_router = lax.psum(router_part, ('seq', 'exp'))]
    all_to_all x0 -> x7, blocking collectives: none -> 126 us  [exchange(): return lax.all_to_all(x, axes, 0, 0, tiled=True)]
    pmax x1 -> x0, blocking collectives: 81.4 us -> none  [per_device(): col_peak = lax.pmax(local_peak, ('seq', 'exp'))]
    all_gather x2 -> x0, blocking collectives: 79 us -> none  [to_tokens(): return lax.all_gather(summed, 'seq', axis=2, tiled=True)]
    dot_general x11 -> x0, matrix products: 43.5 us -> none  [the longest x1 7.17 us: per_device(): jnp.einsum('cns,ds->cnd', d_logit, router, preferred_element_type=jnp.flo...]
    pallas_call x0 -> x11, Pallas kernels: none -> 20.6 us  [call(): pl.pallas_call(body, out_shape=[jax.ShapeDtypeStruct(s, t) for s, t in ou...]
    ppermute x0 -> x4, starting transfers between devices: none -> 13.1 us  [to_partner(): return lax.ppermute(x, 'core', [(0, 1), (1, 0)])]
  transfers between devices with their start and end apart: 1 -> 4, of which waited for: 1 -> 3; matrix products, arithmetic and copies ran while one was open for 2% -> 0% of each run, Pallas kernels for 0% -> 1%
where the time goes in v1:
time: 169 us
  blocking collectives  126 us (75%)
  Pallas kernels  20.6 us (12%)
  starting transfers between devices  13.1 us (8%)
  waiting for transfers between devices  5.93 us (4%)
  local copies, waits for them, and re-layouts  2.52 us (1%)
    all_to_all x7, blocking collectives, exchange(): return lax.all_to_all(x, axes, 0, 0, tiled=True)  126 us
    pallas_call x11, Pallas kernels, call(): pl.pallas_call(body, out_shape=[jax.ShapeDtypeStruct(s, t) for s, t in ou...  20.6 us
    ppermute x4, starting transfers between devices, to_partner(): return lax.ppermute(x, 'core', [(0, 1), (1, 0)])  13.1 us
    ppermute x4, waiting for transfers between devices, to_partner(): return lax.ppermute(x, 'core', [(0, 1), (1, 0)])  5.93 us
  transfers between devices with their start and end apart: 4, of which 3 were waited for; matrix products, arithmetic and copies ran while one was open for 0% of the time, Pallas kernels for 1%

profile of v1, /device:TPU:1, one launch (start us, length us, event | category | flops | bytes accessed | tf_op | source)
XLA Modules:
  0.0 168.7 jit_solution(11540067576313959320)
XLA Ops:
  0.6 0.0 copy-start.2
  0.6 1.5 copy-done.2
  2.2 0.0 copy-start.3
  2.2 1.0 copy-done.3
  3.2 4.8 %shard_map.68 = (bf16[16,24,1408]{2,1,0:T(8,128)(2,1)S(1)}, bf16[16,24,1408]{2,1,0:T(8,128)(2,1)S(1)}, bf16[256,1280]{1,0:T(8,128)(2,1)S(1)}, f32[3,256,256]{2,1,0:T(8,128)S(1)}) custom-call(s32[1]{0:T(128)} %bitcast.core_ref, bf16[3,256,1280]{2,1,0:T(8,128)(2,1)S(1)} %copy-done.2, bf16[1280,128]{1,0:T(8,128)(2,1)S(1)} %copy-done.3, bf16[3,256,1280]{2,1,0:T(8,128)(2,1)} %cot.3), custom_call_target="tpu_custom_call" | custom-call | flops 3000000000 | bytes 8000000 | tf_op jit(solution)/shard_map/pallas_call | solution.py:84
  8.0 3.3 %collective-permute-start = (bf16[16,24,1408]{2,1,0:T(8,128)(2,1)S(1)}, bf16[16,24,1408]{2,1,0:T(8,128)(2,1)S(1)}, u32[]{:S(2)}, u32[]{:S(2)}) collective-permute-start(bf16[16,24,1408]{2,1,0:T(8,128)(2,1)S(1)} %get-tuple-element.15), channel_id=1, source_target_pairs={{0,8},{8,0},{1,9},{9,1},{2,10},{10,2},{3,11},{11,3},{4,12},{12,4},... | collective-permute-start | bytes 3244040 | tf_op jit(solution)/shard_map/ppermute | solution.py:278
  11.3 2.3 %collective-permute-done.b_ref = bf16[16,24,1408]{2,1,0:T(8,128)(2,1)S(1)} collective-permute-done((bf16[16,24,1408]{2,1,0:T(8,128)(2,1)S(1)}, bf16[16,24,1408]{2,1,0:T(8,128)(2,1)S(1)}, u32[]{:S(2)}, u32[]{:S(2)}) %collective-permute-start) | collective-permute-done | bytes 1081376 | tf_op jit(solution)/shard_map/ppermute | solution.py:278
  13.7 0.7 shard_map.69
  14.3 0.0 copy-start
  14.4 36.1 %all_to_all.35.x_ref = bf16[16,24,1408]{2,1,0:T(8,128)(2,1)S(1)} all-to-all(bf16[16,24,1408]{2,1,0:T(8,128)(2,1)S(1)} %shard_map.69), channel_id=1, replica_groups=mesh['yl'=2,'z'=8,'core'=2,'yh'=2,'x'=4] {'yl','z'}, dimensions={0} | all-to-all | bytes 2162688 | tf_op jit(solution)/shard_map/all_to_all | solution.py:274
  50.5 0.4 shard_map.70
  50.9 15.7 %all_to_all.36.x_ref = bf16[8,24,1408]{2,1,0:T(8,128)(2,1)S(1)} all-to-all(bf16[8,24,1408]{2,1,0:T(8,128)(2,1)S(1)} %shard_map.70), channel_id=1, replica_groups=mesh['yl'=2,'z'=8,'core'=2,'yh'=2,'x'=4] {'yh','x'}, dimensions={0} | all-to-all | bytes 1081344 | tf_op jit(solution)/shard_map/all_to_all | solution.py:274
  66.6 0.0 copy-done
  66.6 5.1 %shard_map.71 = (bf16[8,24,1280]{2,1,0:T(8,128)(2,1)S(1)}, f32[24,1408]{1,0:T(8,128)S(1)}) custom-call(bf16[8,24,1408]{2,1,0:T(8,128)(2,1)S(1)} %all_to_all.36.x_ref, bf16[2,1280,640]{2,1,0:T(8,128)(2,1)S(1)} %copy-done, bf16[2,640,1280]{2,1,0:T(8,128)(2,1)} %w_out.1), custom_call_target="tpu_custom_call" | custom-call | flops 1000000000 | bytes 8000000 | tf_op jit(solution)/shard_map/pallas_call | solution.py:84
  71.6 11.4 %all_to_all.37.x_ref = bf16[8,24,1280]{2,1,0:T(8,128)(2,1)S(1)} all-to-all(bf16[8,24,1280]{2,1,0:T(8,128)(2,1)S(1)} %get-tuple-element.16), channel_id=1, replica_groups=mesh['yl'=2,'z'=8,'core'=2,'yh'=2,'x'=4] {'yh','x'}, dimensions={0} | all-to-all | bytes 983040 | tf_op jit(solution)/shard_map/all_to_all | solution.py:274
  83.0 0.2 shard_map.72
  83.2 29.9 %all_to_all.38.gm = bf16[16,24,1408]{2,1,0:T(8,128)(2,1)S(1)} all-to-all(bf16[16,24,1408]{2,1,0:T(8,128)(2,1)S(1)} %shard_map.72), channel_id=1, replica_groups=mesh['yl'=2,'z'=8,'core'=2,'yh'=2,'x'=4] {'yl','z'}, dimensions={0} | all-to-all | bytes 2162688 | tf_op jit(solution)/shard_map/all_to_all | solution.py:274
  113.1 5.6 %collective-permute-start.1 = (bf16[16,24,1408]{2,1,0:T(8,128)(2,1)S(1)}, bf16[16,24,1408]{2,1,0:T(8,128)(2,1)S(1)}, u32[]{:S(2)}, u32[]{:S(2)}) collective-permute-start(bf16[16,24,1408]{2,1,0:T(8,128)(2,1)S(1)} %all_to_all.38.gm), channel_id=1, source_target_pairs={{0,8},{8,0},{1,9},{9,1},{2,10},{10,2},{3,11},{11,3},{4,12},{12,4},... | collective-permute-start | bytes 3244040 | tf_op jit(solution)/shard_map/ppermute | solution.py:278
  118.8 2.3 %collective-permute-done.1.gt = bf16[16,24,1408]{2,1,0:T(8,128)(2,1)S(1)} collective-permute-done((bf16[16,24,1408]{2,1,0:T(8,128)(2,1)S(1)}, bf16[16,24,1408]{2,1,0:T(8,128)(2,1)S(1)}, u32[]{:S(2)}, u32[]{:S(2)}) %collective-permute-start.1) | collective-permute-done | bytes 1081376 | tf_op jit(solution)/shard_map/ppermute | solution.py:278
  121.1 5.2 %shard_map.73 = (f32[16,8,640]{2,1,0:T(8,128)S(1)}, f32[16,8,640]{2,1,0:T(8,128)S(1)}, bf16[3,256,256]{2,1,0:T(8,128)(2,1)S(1)}, bf16[3,256,256]{2,1,0:T(8,128)(2,1)S(1)}, bf16[3,256,1280]{2,1,0:T(8,128)(2,1)}) custom-call(bf16[3,256,1280]{2,1,0:T(8,128)(2,1)} %tokens.3, bf16[3,256,1280]{2,1,0:T(8,128)(2,1)} %cot.3, ...), custom_call_target="tpu_custom_call" | custom-call | flops 3000000000 | bytes 10000000 | tf_op jit(solution)/shard_map/pallas_call | solution.py:84
  126.3 0.4 collective-permute-start.2
  126.7 1.3 collective-permute-done.2.b_ref
  128.0 11.3 %all_to_all.39.x_ref = f32[16,8,640]{2,1,0:T(8,128)S(1)} all-to-all(f32[16,8,640]{2,1,0:T(8,128)S(1)} %shard_map.75), channel_id=1, replica_groups=mesh['yl'=2,'z'=8,'core'=2,'yh'=2,'x'=4] {'yl','yh','x'}, dimensions={0} | all-to-all | bytes 655360 | tf_op jit(solution)/shard_map/all_to_all | solution.py:274
  139.2 0.0 copy-start.1
  139.3 10.9 %all_to_all.40.x_ref = f32[8,8,640]{2,1,0:T(8,128)S(1)} all-to-all(f32[8,8,640]{2,1,0:T(8,128)S(1)} %shard_map.76), channel_id=1, replica_groups=mesh['yl'=2,'z'=8,'core'=2,'yh'=2,'x'=4] {'z'}, dimensions={0} | all-to-all | bytes 327680 | tf_op jit(solution)/shard_map/all_to_all | solution.py:274
  150.2 10.7 %all_to_all.41.mine = f32[16,8,640]{2,1,0:T(8,128)S(1)} all-to-all(f32[16,8,640]{2,1,0:T(8,128)S(1)} %shard_map.77), channel_id=1, replica_groups=mesh['yl'=2,'z'=8,'core'=2,'yh'=2,'x'=4] {'yl','yh','x'}, dimensions={0} | all-to-all | bytes 655360 | tf_op jit(solution)/shard_map/all_to_all | solution.py:274
  160.9 3.7 %collective-permute-start.3 = (f32[16,8,640]{2,1,0:T(8,128)S(1)}, f32[16,8,640]{2,1,0:T(8,128)S(1)}, u32[]{:S(2)}, u32[]{:S(2)}) collective-permute-start(f32[16,8,640]{2,1,0:T(8,128)S(1)} %all_to_all.41.mine), channel_id=1, source_target_pairs={{0,8},{8,0},{1,9},{9,1},{2,10},{10,2},{3,11},{11,3},{4,12},{12,4},... | collective-permute-start | bytes 983048 | tf_op jit(solution)/shard_map/ppermute | solution.py:278
  164.6 0.0 copy-done.1
  164.6 2.5 %shard_map.74 = bf16[3,256,1280]{2,1,0:T(8,128)(2,1)} custom-call(bf16[3,256,256]{2,1,0:T(8,128)(2,1)S(1)} %get-tuple-element.18.dl_ref, bf16[3,256,256]{2,1,0:T(8,128)(2,1)S(1)} %get-tuple-element.19.w_ref, bf16[256,1280]{1,0:T(8,128)(2,1)S(1)} %get-tuple-element.20.rt_ref, bf16[3,256,1280]{2,1,0:T(8,128)(2,1)S(1)} %copy-done.1), custom_call_target="tpu_custom_call" | custom-call | flops 1000000000 | bytes 6000000 | tf_op jit(solution)/shard_map/pallas_call | solution.py:84
  167.1 0.0 collective-permute-done.3.theirs
  167.1 1.7 shard_map.78
  (3 shorter events, 0.1 us)
Async XLA Ops:
  0.6 1.5 copy-start.2
  2.2 1.0 copy-start.3
  8.0 5.7 %collective-permute-start = (bf16[16,24,1408]{2,1,0:T(8,128)(2,1)S(1)}, bf16[16,24,1408]{2,1,0:T(8,128)(2,1)S(1)}, u32[]{:S(2)}, u32[]{:S(2)}) collective-permute-start(bf16[16,24,1408]{2,1,0:T(8,128)(2,1)S(1)} %get-tuple-element.15), channel_id=1, source_target_pairs={{0,8},{8,0},{1,9},{9,1},{2,10},{10,2},{3,11},{11,3},{4,12},{12,4},... | collective-permute-start | bytes 3244040 | tf_op jit(solution)/shard_map/ppermute | solution.py:278
  14.3 52.2 %copy-start = (bf16[2,1280,640]{2,1,0:T(8,128)(2,1)S(1)}, bf16[2,1280,640]{2,1,0:T(8,128)(2,1)}, u32[]{:S(2)}) copy-start(bf16[2,1280,640]{2,1,0:T(8,128)(2,1)} %w_in.1) | copy-start | bytes 9830404
  113.1 8.0 %collective-permute-start.1 = (bf16[16,24,1408]{2,1,0:T(8,128)(2,1)S(1)}, bf16[16,24,1408]{2,1,0:T(8,128)(2,1)S(1)}, u32[]{:S(2)}, u32[]{:S(2)}) collective-permute-start(bf16[16,24,1408]{2,1,0:T(8,128)(2,1)S(1)} %all_to_all.38.gm), channel_id=1, source_target_pairs={{0,8},{8,0},{1,9},{9,1},{2,10},{10,2},{3,11},{11,3},{4,12},{12,4},... | collective-permute-start | bytes 3244040 | tf_op jit(solution)/shard_map/ppermute | solution.py:278
  126.3 1.6 collective-permute-start.2
  139.2 25.4 %copy-start.1 = (bf16[3,256,1280]{2,1,0:T(8,128)(2,1)S(1)}, bf16[3,256,1280]{2,1,0:T(8,128)(2,1)}, u32[]{:S(2)}) copy-start(bf16[3,256,1280]{2,1,0:T(8,128)(2,1)} %get-tuple-element.21.g_ref) | copy-start | bytes 5898244
  160.9 6.2 %collective-permute-start.3 = (f32[16,8,640]{2,1,0:T(8,128)S(1)}, f32[16,8,640]{2,1,0:T(8,128)S(1)}, u32[]{:S(2)}, u32[]{:S(2)}) collective-permute-start(f32[16,8,640]{2,1,0:T(8,128)S(1)} %all_to_all.41.mine), channel_id=1, source_target_pairs={{0,8},{8,0},{1,9},{9,1},{2,10},{10,2},{3,11},{11,3},{4,12},{12,4},... | collective-permute-start | bytes 983048 | tf_op jit(solution)/shard_map/ppermute | solution.py:278

commit v2 on v1

v2 whole, which is shorter than its diff:
```python
import functools

import jax
import jax.numpy as jnp
from jax import lax
from jax.experimental import pallas as pl
from jax.experimental.pallas import tpu as pltpu
from jax.sharding import Mesh, PartitionSpec as P

SIZES = {"yl": 2, "z": 8, "core": 2, "yh": 2, "x": 4}
AXES = tuple(SIZES)
OWNERS = ("yl", "z")
EXP = ("yh", "x")
PLANE = ("yl", "yh", "x")

D = 1280
CLIPS = 3
TOK = 256
ROWS = 24
PART = 512
STAT = 96
MiB = 1024 * 1024
GELU_C = 0.7978845608028654
GELU_A = 0.044715

bf16 = jnp.bfloat16
f32 = jnp.float32

NT = (((1,), (1,)), ((), ()))
TN = (((0,), (0,)), ((), ()))


def dot(a, b, dims=None):
    if dims is None:
        return jnp.dot(a, b, preferred_element_type=f32)
    return lax.dot_general(a, b, dims, preferred_element_type=f32)


def is_grad_row(shape):
    return lax.broadcasted_iota(jnp.int32, shape, 0) % 8 >= 4


def swap_halves(v, grad):
    n = v.shape[0]
    return jnp.where(grad, pltpu.roll(v, 4, 0), pltpu.roll(v, n - 4, 0))


def lanes_of(shape):
    return lax.broadcasted_iota(jnp.int32, shape, len(shape) - 1)


def split(value):
    high = value.astype(bf16).astype(f32)
    rest = value - high
    middle = rest.astype(bf16).astype(f32)
    return high, middle, rest - middle


def spread_triple(value):
    high, middle, low = split(value)
    return high + pltpu.roll(middle, 1, 1) + pltpu.roll(low, 2, 1)


def join_triple(stats):
    return stats + pltpu.roll(stats, 127, 1) + pltpu.roll(stats, 126, 1)


def clip_columns(x):
    return [x[:, STAT + 8 * c : STAT + 8 * c + 1] for c in range(CLIPS)]


def by_quarter(columns, lane):
    first = jnp.where(lane < 32, columns[0], columns[1])
    return jnp.where(lane < 64, first, columns[2])


def merge_stats(last):
    joined = [join_triple(x) for x in last]
    peak = functools.reduce(jnp.maximum, joined)
    scales = [jnp.exp(jnp.minimum(j - peak, 0.0)) for j in joined]
    total = functools.reduce(jnp.add, [pltpu.roll(x, 3, 1) * j for x, j in zip(scales, joined)])
    lane = lanes_of(peak.shape)
    stats = jnp.where(lane % 8 == 0, peak, jnp.where(lane % 8 == 3, total, 0.0))
    stats = spread_triple(jnp.where(lane < STAT, 0.0, stats))
    return [clip_columns(x) for x in scales], stats


def merge_tiles(wide, columns, stats):
    tiles = []
    for c in range(CLIPS):
        lanes = slice(128 * c, 128 * c + 128)
        parts = [col[c] * b[:, lanes] for b, col in zip(wide, columns)]
        tiles.append(functools.reduce(jnp.add, parts))
    lane = lanes_of(stats.shape)
    parts = [by_quarter(col, lane) * b[:, 384:] for b, col in zip(wide, columns)]
    tiles.append(jnp.where(lane < STAT, functools.reduce(jnp.add, parts), stats))
    return jnp.concatenate(tiles, axis=1)


def merge_blocks(blocks):
    wide = [b.astype(f32) for b in blocks]
    return merge_tiles(wide, *merge_stats([b[:, 384:] for b in wide]))


def rows_of(blocks, c):
    lane = lanes_of((blocks[0].shape[0], 128))
    tiles = [b[:, 128 * c : 128 * c + 128] for b in blocks]
    for first in (0, 4):
        tile = None
        for q in range(4):
            turned = blocks[first + q][:, 384:]
            if q != c:
                turned = pltpu.roll(turned, 32 * (q - c) % 128, 1)
            tile = turned if tile is None else jnp.where(lane // 32 == q, turned, tile)
        tiles.append(tile)
    return jnp.concatenate(tiles, axis=1)


def last_tile(tails, j, stats):
    lane = lanes_of(stats.shape)
    out = stats
    for c, tail in enumerate(tails):
        tile = tail[:, 128 * (j // 4) : 128 * (j // 4) + 128]
        if j % 4 != c:
            tile = pltpu.roll(tile, 32 * (c - j % 4) % 128, 1)
        out = jnp.where(lane // 32 == c, tile, out)
    return out


def call(body, outs, *args, scratch=(), flops=0, nbytes=0, smem=(), hbm=(), limit=16):
    spaces = [
        pltpu.SMEM if i in smem else pltpu.HBM if i in hbm else pltpu.VMEM for i in range(len(args))
    ]
    return pl.pallas_call(
        body,
        out_shape=[jax.ShapeDtypeStruct(s, t) for s, t in outs],
        in_specs=[pl.BlockSpec(memory_space=s) for s in spaces],
        out_specs=[pl.BlockSpec(memory_space=pltpu.VMEM) for _ in outs],
        scratch_shapes=list(scratch),
        compiler_params=pltpu.CompilerParams(vmem_limit_bytes=limit * MiB),
        cost_estimate=pl.CostEstimate(flops=flops, bytes_accessed=nbytes, transcendentals=0),
    )(*args)


def slot_of_row(core):
    t = lax.broadcasted_iota(jnp.int32, (256, 128), 0)
    s = lax.broadcasted_iota(jnp.int32, (256, 128), 1)
    half = t // 128
    slot = 8 * ((t % 128) // 8) + 4 * (half + core * (1 - 2 * half)) + t % 4
    return s == slot, t


def slots_body(
    core_ref, router_hbm, tokens_hbm, cot_hbm, mine, theirs, rt_ref, lt_ref,
    router, tokens, cot, weights_in, weights_out, sems, router_sem,
):
    first = pltpu.make_async_copy(router_hbm, router, router_sem)
    copies = [
        pltpu.make_async_copy(src.at[c], dst.at[c], sems.at[i, c])
        for i, (src, dst) in enumerate(((tokens_hbm, tokens), (cot_hbm, cot)))
        for c in range(CLIPS)
    ]
    first.start()
    for copy in copies:
        copy.start()
    pick, _ = slot_of_row(core_ref[0])
    pick = pick.astype(f32).astype(bf16)
    first.wait()
    rt_ref[...] = dot(pick, router[...], NT).astype(bf16)
    grad = is_grad_row((256, TOK))
    lane = lanes_of((256, 128))
    stats = jnp.zeros((256, 128), f32)
    for c in range(CLIPS):
        copies[c].wait()
        logits = dot(rt_ref[...], tokens[c], NT)
        lt_ref[c] = logits
        peak = jnp.max(logits, axis=1, keepdims=True)
        low = jnp.where(grad, 0.0, jnp.exp(logits - peak)).astype(bf16)
        total = jnp.sum(low.astype(f32), axis=1, keepdims=True)
        weights_in[c] = low
        raised = jnp.exp(logits - jnp.max(logits, axis=0, keepdims=True))
        combine = raised * (2.0 / jnp.sum(raised, axis=0, keepdims=True))
        weights_out[c] = jnp.where(grad, combine, 0.0).astype(bf16)
        at = STAT + 8 * c
        stats = jnp.where(lane == at, peak, jnp.where(lane == at + 3, total, stats))
    ones = jnp.where((lane >= STAT) & (lane % 8 == 3), 1.0, 0.0)
    stats = spread_triple(jnp.where(is_grad_row((256, 128)), ones, stats))

    def product(c, lanes):
        return dot(weights_in[c], tokens[c, :, lanes]) + dot(weights_out[c], cot[c, :, lanes])

    for c in range(CLIPS):
        copies[CLIPS + c].wait()
        for i in range(4):
            part = product(c, slice(256 * i, 256 * i + 256)).reshape(32, 8, 256)
            for h in range(2):
                tile = part[:, :, 128 * h : 128 * h + 128]
                mine[2 * i + h, :, :, 128 * c : 128 * c + 128] = tile[:16]
                theirs[2 * i + h, :, :, 128 * c : 128 * c + 128] = tile[16:].astype(bf16)
    tails = [product(c, slice(1024, 1280)) for c in range(CLIPS)]
    for j in range(8):
        tile = last_tile(tails, j, stats).reshape(32, 8, 128)
        mine[j, :, :, 384:] = tile[:16]
        theirs[j, :, :, 384:] = tile[16:].astype(bf16)


def pair_body(a_ref, b_ref, out):
    columns, stats = merge_stats([x[0, :, :, 384:].astype(f32).reshape(128, 128) for x in (a_ref, b_ref)])
    for j in range(8):
        wide = [x[j].astype(f32).reshape(128, PART) for x in (a_ref, b_ref)]
        out[j] = merge_tiles(wide, columns, stats).astype(bf16).reshape(16, 8, PART)


def members_body(x_ref, out):
    blocks = [x_ref[e].astype(f32).reshape(128, PART) for e in range(8)]
    out[...] = merge_blocks(blocks).reshape(16, 8, PART)


def owner_body(x_ref, out, own):
    merged = merge_blocks([x_ref[d] for d in range(16)])
    last = merged[:, 384:]
    joined = join_triple(last)
    grad = is_grad_row((8, 1))
    totals = [joined[:, STAT + 8 * c + 3 : STAT + 8 * c + 4] for c in range(CLIPS)]
    inverse = [jnp.where(grad, 1.0, 1.0 / total) for total in totals]
    lane = lanes_of(last.shape)
    tiles = [merged[:, 128 * c : 128 * c + 128] * inverse[c] for c in range(CLIPS)]
    tiles.append(jnp.where(lane < STAT, last * by_quarter(inverse, lane), last))
    rows = jnp.concatenate(tiles, axis=1)
    own[...] = rows
    low = rows.astype(bf16)
    for e in range(8):
        out[e] = low


def gelu_parts(v):
    t = jnp.tanh(GELU_C * (v + GELU_A * (v * v * v)))
    value = 0.5 * v * (1.0 + t)
    slope = 0.5 * (1.0 + t) + 0.5 * v * (1.0 - t * t) * (GELU_C * (1.0 + 3.0 * GELU_A * (v * v)))
    return value, slope


def expert_body(x_ref, w_in, w_out, out, stats_out):
    blocks = [x_ref[e].astype(f32) for e in range(8)]
    stats_out[...] = join_triple(blocks[0][:, 384:])
    low = jnp.concatenate([rows_of(blocks, c) for c in range(CLIPS)], axis=0).astype(bf16)
    row = lax.broadcasted_iota(jnp.int32, (ROWS, 640), 0)
    grad = row % 8 >= 4
    acc = jnp.zeros((ROWS, D), f32)
    for i in range(2):
        own = (row % 4) // 2 == i
        value, slope = gelu_parts(dot(low, w_in[i]))
        d_pre = dot(low, w_out[i], NT) * pltpu.roll(slope, 4, 0)
        hidden = jnp.where(own & jnp.logical_not(grad), value, 0.0).astype(bf16)
        d_pre = jnp.where(own & grad, d_pre, 0.0).astype(bf16)
        acc = acc + dot(hidden, w_out[i]) + dot(d_pre, w_in[i], NT)
    by_clip = [acc[8 * c : 8 * c + 8] for c in range(CLIPS)]
    tails = [rows[:, 1024:] for rows in by_clip]
    empty = jnp.zeros((8, 128), f32)
    for j in range(8):
        tiles = [rows[:, 128 * j : 128 * j + 128] for rows in by_clip]
        out[j] = jnp.concatenate(tiles + [last_tile(tails, j, empty)], axis=1)


def result_body(x_ref, joined, own, out):
    acc = x_ref[0]
    for e in range(1, 8):
        acc = acc + x_ref[e]
    low = acc.astype(bf16).astype(f32)
    products = low * pltpu.roll(own[...], 4, 0)
    lane = lanes_of((8, 128))
    grad = is_grad_row((8, 128))
    kept = jnp.where((lane % 8 == 0) | (lane % 8 == 3), joined[...], 0.0)
    dots = jnp.zeros((8, 128), f32)
    for c in range(CLIPS):
        both = products[:, 128 * c : 128 * c + 128]
        both = both + jnp.where(lane // 32 == c, products[:, 384:], 0.0)
        total = jnp.sum(both, axis=1, keepdims=True)
        dots = jnp.where(lane == STAT + 8 * c, total, dots)
    stats = spread_triple(jnp.where(lane < STAT, 0.0, jnp.where(grad, dots, kept)))
    last = jnp.where(lane < STAT, low[:, 384:], stats)
    full = jnp.concatenate([low[:, :384], last], axis=1).astype(bf16)
    for d in range(16):
        out[d] = full


def copies_body(x_ref, out):
    for e in range(8):
        out[e] = x_ref[...]


def logit_body(tokens, cot, lt_ref, gm, gt, r_mine, r_theirs, dl_ref, w_ref, g_ref, r_sum):
    grad = is_grad_row((256, TOK))
    grad_half = is_grad_row((256, 640))
    halves = [[g[j].astype(f32).reshape(128, PART) for j in range(8)] for g in (gm, gt)]
    dots = [functools.reduce(jnp.add, [part[:, 384:] for part in h]) for h in halves]
    dots = join_triple(jnp.concatenate(dots, axis=0))
    stats = join_triple(jnp.concatenate([h[0][:, 384:] for h in halves], axis=0))
    stats = pltpu.roll(stats, 4, 0)
    for c in range(CLIPS):
        low = jnp.concatenate([rows_of(h, c).astype(bf16) for h in halves], axis=0)
        g_ref[c] = low
        at = STAT + 8 * c
        peak = stats[:, at : at + 1]
        total = stats[:, at + 3 : at + 4]
        column_dot = dots[:, at : at + 1]
        logits = lt_ref[c]
        raised = jnp.exp(logits - jnp.max(logits, axis=0, keepdims=True))
        combine = raised * (2.0 / jnp.sum(raised, axis=0, keepdims=True))
        combine = jnp.where(grad, 0.0, combine)
        d_combine = dot(low, cot[c], NT)
        inner = jnp.sum(combine * d_combine, axis=0, keepdims=True)
        dispatch = jnp.where(grad, jnp.exp(logits - peak) * (1.0 / total), 0.0)
        d_dispatch = dot(low, tokens[c], NT)
        own = jnp.where(grad, dispatch * (d_dispatch - column_dot), combine * (d_combine - inner))
        d_logit = (own + swap_halves(own, grad)).astype(bf16)
        part = dot(d_logit, tokens[c])
        part = jnp.where(grad_half, part[:, 640:], part[:, :640])
        if c == 0:
            r_sum[...] = part
        else:
            r_sum[...] += part
        dl_ref[c] = jnp.where(grad, 0.0, d_logit.astype(f32)).astype(bf16)
        w_ref[c] = dispatch.astype(bf16)
    r_mine[...] = r_sum[:128].astype(bf16).reshape(16, 8, 640)
    r_theirs[...] = r_sum[128:].astype(bf16).reshape(16, 8, 640)


def tokens_body(dl_ref, w_ref, rt_ref, g_ref, out):
    for c in range(CLIPS):
        out[c] = (dot(dl_ref[c], rt_ref[...], TN) + dot(w_ref[c], g_ref[c], TN)).astype(bf16)


def add_body(a_ref, b_ref, out):
    out[...] = (a_ref[...].astype(f32) + b_ref[...].astype(f32)).astype(bf16)


def spread_body(x_ref, out):
    acc = x_ref[0].astype(f32)
    for i in range(1, x_ref.shape[0]):
        acc = acc + x_ref[i].astype(f32)
    acc = acc.astype(bf16)
    for i in range(out.shape[0]):
        out[i] = acc


def router_body(core_ref, mine, theirs, out):
    hit, t = slot_of_row(core_ref[0])
    rows = [x[...].astype(f32).reshape(128, 640) for x in (mine, theirs)]
    rows = jnp.concatenate(rows, axis=0).astype(bf16)
    for a in range(2):
        pick = (hit & ((t % 8) // 4 == a)).astype(f32).astype(bf16)
        out[a * 640 : (a + 1) * 640, :] = dot(rows, pick, TN)


def exchange(x, axes):
    return lax.all_to_all(x, axes, 0, 0, tiled=True)


def to_partner(x):
    return lax.ppermute(x, "core", [(0, 1), (1, 0)])


def per_device(tokens, router, w_in, w_out, cotangent):
    core = lax.axis_index("core").astype(jnp.int32).reshape(1)
    values = ((8, 16, 8, PART), bf16)
    local = (CLIPS, TOK, D)
    square = ((CLIPS, 256, TOK), bf16)
    mine, theirs, rt, lt = call(
        slots_body,
        [(values[0], f32), values, ((256, D), bf16), ((CLIPS, 256, TOK), f32)],
        core,
        *[pltpu.with_memory_space_constraint(x, pltpu.HBM) for x in (router, tokens, cotangent)],
        scratch=[
            pltpu.VMEM((D, 128), bf16),
            pltpu.VMEM(local, bf16),
            pltpu.VMEM(local, bf16),
            pltpu.VMEM(*square),
            pltpu.VMEM(*square),
            pltpu.SemaphoreType.DMA((2, CLIPS)),
            pltpu.SemaphoreType.DMA,
        ],
        smem=(0,),
        hbm=(1, 2, 3),
        flops=3 * 10**9,
        nbytes=8 * 10**6,
        limit=24,
    )
    (sums,) = call(pair_body, [values], mine, to_partner(theirs), flops=10**10, nbytes=3 * 10**6)
    (sums,) = call(
        members_body, [((16, 8, PART), f32)], exchange(sums, EXP), flops=10**10, nbytes=10**6
    )
    sums, own = call(
        owner_body,
        [((8, 8, PART), bf16), ((8, PART), f32)],
        exchange(sums, OWNERS),
        nbytes=10**5,
    )
    parts, stats = call(
        expert_body,
        [((8, 8, PART), f32), ((8, 128), f32)],
        exchange(sums, EXP),
        w_in,
        w_out,
        flops=10**9,
        nbytes=8 * 10**6,
    )
    (result,) = call(
        result_body, [((16, 8, PART), bf16)], exchange(parts, EXP), stats, own, nbytes=10**5
    )
    (result,) = call(copies_body, [values], exchange(result, OWNERS), nbytes=10**6)
    g_mine = exchange(result, EXP)
    g_theirs = to_partner(g_mine)
    half = ((16, 8, 640), bf16)
    r_mine, r_theirs, d_logit, dispatch, grads = call(
        logit_body,
        [half, half, square, square, (local, bf16)],
        tokens,
        cotangent,
        lt,
        g_mine,
        g_theirs,
        scratch=[pltpu.VMEM((256, 640), f32)],
        flops=3 * 10**9,
        nbytes=10**7,
        limit=24,
    )
    (r_mine,) = call(add_body, [half], r_mine, to_partner(r_theirs), nbytes=10**6)
    (d_tokens,) = call(
        tokens_body, [(local, bf16)], d_logit, dispatch, rt, grads, flops=10**9, nbytes=6 * 10**6
    )
    r_mine = exchange(r_mine, PLANE)
    (r_mine,) = call(spread_body, [((8, 8, 640), bf16)], r_mine, nbytes=10**5)
    r_mine = exchange(r_mine, ("z",))
    (r_mine,) = call(spread_body, [half], r_mine, nbytes=10**5)
    r_mine = exchange(r_mine, PLANE)
    (d_router,) = call(
        router_body, [((D, 128), f32)], core, r_mine, to_partner(r_mine), smem=(0,), nbytes=2 * 10**6
    )
    return (d_tokens, d_router)


def solution(mesh):
    fine = Mesh(mesh.devices.reshape(tuple(SIZES.values())), AXES)
    seq = ("yl", "z", "core")
    placed = (
        P(None, AXES, None),
        P(),
        P(seq, None, EXP),
        P(seq, EXP, None),
        P(None, AXES, None),
    )
    return jax.shard_map(
        per_device,
        mesh=fine,
        in_specs=placed,
        out_specs=(P(None, AXES, None), P()),
        check_vma=False,
    )
```

time: 169 us -> 154 us (0.911)
  blocking collectives: 126 us -> 115 us
  local copies, waits for them, and re-layouts: 2.52 us -> 0.02 us
  Pallas kernels: 20.6 us -> 18.7 us
    all_to_all x7 -> x9, blocking collectives: 126 us -> 115 us  [exchange(): return lax.all_to_all(x, axes, 0, 0, tiled=True)]
    unnamed x8, local copies, waits for them, and re-layouts: 2.52 us -> 0.02 us
    pallas_call x11 -> x13, Pallas kernels: 20.6 us -> 18.7 us  [call(): pl.pallas_call(body, out_shape=[jax.ShapeDtypeStruct(s, t) for s, t in ou...]
  transfers between devices with their start and end apart: 4 -> 4, of which waited for: 3 -> 3; matrix products, arithmetic and copies ran while one was open for 0% -> 0% of each run, Pallas kernels for 1% -> 2%
where the time goes in v2:
time: 154 us
  blocking collectives  115 us (75%)
  Pallas kernels  18.7 us (12%)
  starting transfers between devices  14.2 us (9%)
  waiting for transfers between devices  5.6 us (4%)
    all_to_all x9, blocking collectives, exchange(): return lax.all_to_all(x, axes, 0, 0, tiled=True)  115 us
    pallas_call x13, Pallas kernels, call(): pl.pallas_call(body, out_shape=[jax.ShapeDtypeStruct(s, t) for s, t in ou...  18.7 us
    ppermute x4, starting transfers between devices, to_partner(): return lax.ppermute(x, 'core', [(0, 1), (1, 0)])  14.2 us
    ppermute x4, waiting for transfers between devices, to_partner(): return lax.ppermute(x, 'core', [(0, 1), (1, 0)])  5.6 us
  transfers between devices with their start and end apart: 4, of which 3 were waited for; matrix products, arithmetic and copies ran while one was open for 0% of the time, Pallas kernels for 2%

profile of v2, /device:TPU:1, one launch (start us, length us, event | category | flops | bytes accessed | tf_op | source)
XLA Modules:
  0.0 153.9 jit_solution(1058118279699279239)
XLA Ops:
  0.6 6.7 %shard_map.68 = (f32[8,16,8,512]{3,2,1,0:T(8,128)S(1)}, bf16[8,16,8,512]{3,2,1,0:T(8,128)(2,1)S(1)}, bf16[256,1280]{1,0:T(8,128)(2,1)S(1)}, f32[3,256,256]{2,1,0:T(8,128)S(1)}) custom-call(s32[1]{0:T(128)} %bitcast.core_ref, bf16[1280,128]{1,0:T(8,128)(2,1)} %router_hbm.1, bf16[3,256,1280]{2,1,0:T(8,128)(2,1)} %tokens.1, bf16[3,256,1280]{2,1,0:T(8,128)(2,1)} %cot.1), custom_call_target="tpu_custom_call" | custom-call | flops 3000000000 | bytes 8000000 | tf_op jit(solution)/shard_map/pallas_call | solution.py:134
  7.4 3.3 %collective-permute-start = (bf16[8,16,8,512]{3,2,1,0:T(8,128)(2,1)S(1)}, bf16[8,16,8,512]{3,2,1,0:T(8,128)(2,1)S(1)}, u32[]{:S(2)}, u32[]{:S(2)}) collective-permute-start(bf16[8,16,8,512]{3,2,1,0:T(8,128)(2,1)S(1)} %get-tuple-element.17), channel_id=1, source_target_pairs={{0,8},{8,0},{1,9},{9,1},{2,10},{10,2},{3,11},{11,3},{4,12},{12,4},... | collective-permute-start | bytes 3145736 | tf_op jit(solution)/shard_map/ppermute | solution.py:361
  10.7 2.3 %collective-permute-done.b_ref = bf16[8,16,8,512]{3,2,1,0:T(8,128)(2,1)S(1)} collective-permute-done((bf16[8,16,8,512]{3,2,1,0:T(8,128)(2,1)S(1)}, bf16[8,16,8,512]{3,2,1,0:T(8,128)(2,1)S(1)}, u32[]{:S(2)}, u32[]{:S(2)}) %collective-permute-start) | collective-permute-done | bytes 1048608 | tf_op jit(solution)/shard_map/ppermute | solution.py:361
  13.0 0.8 shard_map.69
  13.7 21.3 %all_to_all.45.x_ref = bf16[8,16,8,512]{3,2,1,0:T(8,128)(2,1)S(1)} all-to-all(bf16[8,16,8,512]{3,2,1,0:T(8,128)(2,1)S(1)} %shard_map.69), channel_id=1, replica_groups=mesh['yl'=2,'z'=8,'core'=2,'yh'=2,'x'=4] {'yh','x'}, dimensions={0} | all-to-all | bytes 2097152 | tf_op jit(solution)/shard_map/all_to_all | solution.py:357
  35.0 0.0 copy-start
  35.0 0.0 copy-start.1
  35.0 1.0 shard_map.70
  36.0 16.2 %all_to_all.46.x_ref = f32[16,8,512]{2,1,0:T(8,128)S(1)} all-to-all(f32[16,8,512]{2,1,0:T(8,128)S(1)} %shard_map.70), channel_id=1, replica_groups=mesh['yl'=2,'z'=8,'core'=2,'yh'=2,'x'=4] {'yl','z'}, dimensions={0} | all-to-all | bytes 524288 | tf_op jit(solution)/shard_map/all_to_all | solution.py:357
  52.3 0.4 shard_map.71
  52.7 9.8 %all_to_all.47.x_ref = bf16[8,8,512]{2,1,0:T(8,128)(2,1)S(1)} all-to-all(bf16[8,8,512]{2,1,0:T(8,128)(2,1)S(1)} %get-tuple-element.18), channel_id=1, replica_groups=mesh['yl'=2,'z'=8,'core'=2,'yh'=2,'x'=4] {'yh','x'}, dimensions={0} | all-to-all | bytes 131072 | tf_op jit(solution)/shard_map/all_to_all | solution.py:357
  62.5 0.0 copy-done
  62.5 0.0 copy-done.1
  62.5 3.1 %shard_map.72 = (f32[8,8,512]{2,1,0:T(8,128)S(1)}, f32[8,128]{1,0:T(8,128)S(1)}) custom-call(bf16[8,8,512]{2,1,0:T(8,128)(2,1)S(1)} %all_to_all.47.x_ref, bf16[2,1280,640]{2,1,0:T(8,128)(2,1)S(1)} %copy-done, bf16[2,640,1280]{2,1,0:T(8,128)(2,1)S(1)} %copy-done.1), custom_call_target="tpu_custom_call" | custom-call | flops 1000000000 | bytes 8000000 | tf_op jit(solution)/shard_map/pallas_call | solution.py:134
  65.6 0.0 copy-start.3
  65.6 9.5 %all_to_all.48.x_ref = f32[8,8,512]{2,1,0:T(8,128)S(1)} all-to-all(f32[8,8,512]{2,1,0:T(8,128)S(1)} %get-tuple-element.19), channel_id=1, replica_groups=mesh['yl'=2,'z'=8,'core'=2,'yh'=2,'x'=4] {'yh','x'}, dimensions={0} | all-to-all | bytes 262144 | tf_op jit(solution)/shard_map/all_to_all | solution.py:357
  75.1 0.0 copy-start.2
  75.1 0.2 shard_map.73
  75.2 13.0 %all_to_all.49.x_ref = bf16[16,8,512]{2,1,0:T(8,128)(2,1)S(1)} all-to-all(bf16[16,8,512]{2,1,0:T(8,128)(2,1)S(1)} %shard_map.73), channel_id=1, replica_groups=mesh['yl'=2,'z'=8,'core'=2,'yh'=2,'x'=4] {'yl','z'}, dimensions={0} | all-to-all | bytes 262144 | tf_op jit(solution)/shard_map/all_to_all | solution.py:357
  88.3 0.1 shard_map.74
  88.3 15.2 %all_to_all.50.gm = bf16[8,16,8,512]{3,2,1,0:T(8,128)(2,1)S(1)} all-to-all(bf16[8,16,8,512]{3,2,1,0:T(8,128)(2,1)S(1)} %shard_map.74), channel_id=1, replica_groups=mesh['yl'=2,'z'=8,'core'=2,'yh'=2,'x'=4] {'yh','x'}, dimensions={0} | all-to-all | bytes 2097152 | tf_op jit(solution)/shard_map/all_to_all | solution.py:357
  103.5 6.1 %collective-permute-start.1 = (bf16[8,16,8,512]{3,2,1,0:T(8,128)(2,1)S(1)}, bf16[8,16,8,512]{3,2,1,0:T(8,128)(2,1)S(1)}, u32[]{:S(2)}, u32[]{:S(2)}) collective-permute-start(bf16[8,16,8,512]{3,2,1,0:T(8,128)(2,1)S(1)} %all_to_all.50.gm), channel_id=1, source_target_pairs={{0,8},{8,0},{1,9},{9,1},{2,10},{10,2},{3,11},{11,3},{4,12},{12,4},... | collective-permute-start | bytes 3145736 | tf_op jit(solution)/shard_map/ppermute | solution.py:361
  109.7 2.3 %collective-permute-done.1.gt = bf16[8,16,8,512]{3,2,1,0:T(8,128)(2,1)S(1)} collective-permute-done((bf16[8,16,8,512]{3,2,1,0:T(8,128)(2,1)S(1)}, bf16[8,16,8,512]{3,2,1,0:T(8,128)(2,1)S(1)}, u32[]{:S(2)}, u32[]{:S(2)}) %collective-permute-start.1) | collective-permute-done | bytes 1048608 | tf_op jit(solution)/shard_map/ppermute | solution.py:361
  111.9 0.0 copy-done.3
  112.0 0.0 copy-done.2
  112.0 2.7 %shard_map.75 = (bf16[16,8,640]{2,1,0:T(8,128)(2,1)S(1)}, bf16[16,8,640]{2,1,0:T(8,128)(2,1)S(1)}, bf16[3,256,256]{2,1,0:T(8,128)(2,1)S(1)}, bf16[3,256,256]{2,1,0:T(8,128)(2,1)S(1)}, bf16[3,256,1280]{2,1,0:T(8,128)(2,1)S(1)}) custom-call(bf16[3,256,1280]{2,1,0:T(8,128)(2,1)S(1)} %copy-done.2, bf16[3,256,1280]{2,1,0:T(8,128)(2,1)S(1)} %copy-done.3, ...), custom_call_target="tpu_custom_call" | custom-call | flops 3000000000 | bytes 10000000 | tf_op jit(solution)/shard_map/pallas_call | solution.py:134
  114.7 0.6 collective-permute-start.2
  115.3 1.0 collective-permute-done.2.b_ref
  116.4 9.6 %all_to_all.51.x_ref = bf16[16,8,640]{2,1,0:T(8,128)(2,1)S(1)} all-to-all(bf16[16,8,640]{2,1,0:T(8,128)(2,1)S(1)} %shard_map.77), channel_id=1, replica_groups=mesh['yl'=2,'z'=8,'core'=2,'yh'=2,'x'=4] {'yl','yh','x'}, dimensions={0} | all-to-all | bytes 327680 | tf_op jit(solution)/shard_map/all_to_all | solution.py:357
  126.0 10.1 %all_to_all.52.x_ref = bf16[8,8,640]{2,1,0:T(8,128)(2,1)S(1)} all-to-all(bf16[8,8,640]{2,1,0:T(8,128)(2,1)S(1)} %shard_map.78), channel_id=1, replica_groups=mesh['yl'=2,'z'=8,'core'=2,'yh'=2,'x'=4] {'z'}, dimensions={0} | all-to-all | bytes 163840 | tf_op jit(solution)/shard_map/all_to_all | solution.py:357
  136.2 9.8 %all_to_all.53.mine = bf16[16,8,640]{2,1,0:T(8,128)(2,1)S(1)} all-to-all(bf16[16,8,640]{2,1,0:T(8,128)(2,1)S(1)} %shard_map.79), channel_id=1, replica_groups=mesh['yl'=2,'z'=8,'core'=2,'yh'=2,'x'=4] {'yl','yh','x'}, dimensions={0} | all-to-all | bytes 327680 | tf_op jit(solution)/shard_map/all_to_all | solution.py:357
  146.0 4.1 %collective-permute-start.3 = (bf16[16,8,640]{2,1,0:T(8,128)(2,1)S(1)}, bf16[16,8,640]{2,1,0:T(8,128)(2,1)S(1)}, u32[]{:S(2)}, u32[]{:S(2)}) collective-permute-start(bf16[16,8,640]{2,1,0:T(8,128)(2,1)S(1)} %all_to_all.53.mine), channel_id=1, source_target_pairs={{0,8},{8,0},{1,9},{9,1},{2,10},{10,2},{3,11},{11,3},{4,12},{12,4},... | collective-permute-start | bytes 491528 | tf_op jit(solution)/shard_map/ppermute | solution.py:361
  150.1 2.5 %shard_map.76 = bf16[3,256,1280]{2,1,0:T(8,128)(2,1)} custom-call(bf16[3,256,256]{2,1,0:T(8,128)(2,1)S(1)} %get-tuple-element.22.dl_ref, bf16[3,256,256]{2,1,0:T(8,128)(2,1)S(1)} %get-tuple-element.23.w_ref, bf16[256,1280]{1,0:T(8,128)(2,1)S(1)} %get-tuple-element.24.rt_ref, bf16[3,256,1280]{2,1,0:T(8,128)(2,1)S(1)} %get-tuple-element.25.g_ref), custom_call_target="tpu_custom_call" | custom-call | flops 1000000000 | bytes 6000000 | tf_op jit(solution)/shard_map/pallas_call | solution.py:134
  152.6 0.0 collective-permute-done.3.theirs
  152.6 1.3 shard_map.80
  (3 shorter events, 0.1 us)
Async XLA Ops:
  7.4 5.6 %collective-permute-start = (bf16[8,16,8,512]{3,2,1,0:T(8,128)(2,1)S(1)}, bf16[8,16,8,512]{3,2,1,0:T(8,128)(2,1)S(1)}, u32[]{:S(2)}, u32[]{:S(2)}) collective-permute-start(bf16[8,16,8,512]{3,2,1,0:T(8,128)(2,1)S(1)} %get-tuple-element.17), channel_id=1, source_target_pairs={{0,8},{8,0},{1,9},{9,1},{2,10},{10,2},{3,11},{11,3},{4,12},{12,4},... | collective-permute-start | bytes 3145736 | tf_op jit(solution)/shard_map/ppermute | solution.py:361
  35.0 27.5 %copy-start = (bf16[2,1280,640]{2,1,0:T(8,128)(2,1)S(1)}, bf16[2,1280,640]{2,1,0:T(8,128)(2,1)}, u32[]{:S(2)}) copy-start(bf16[2,1280,640]{2,1,0:T(8,128)(2,1)} %w_in.1) | copy-start | bytes 9830404
  35.0 27.5 %copy-start.1 = (bf16[2,640,1280]{2,1,0:T(8,128)(2,1)S(1)}, bf16[2,640,1280]{2,1,0:T(8,128)(2,1)}, u32[]{:S(2)}) copy-start(bf16[2,640,1280]{2,1,0:T(8,128)(2,1)} %w_out.1) | copy-start | bytes 9830404
  65.6 46.4 %copy-start.3 = (bf16[3,256,1280]{2,1,0:T(8,128)(2,1)S(1)}, bf16[3,256,1280]{2,1,0:T(8,128)(2,1)}, u32[]{:S(2)}) copy-start(bf16[3,256,1280]{2,1,0:T(8,128)(2,1)} %cot.1) | copy-start | bytes 5898244
  75.1 36.9 %copy-start.2 = (bf16[3,256,1280]{2,1,0:T(8,128)(2,1)S(1)}, bf16[3,256,1280]{2,1,0:T(8,128)(2,1)}, u32[]{:S(2)}) copy-start(bf16[3,256,1280]{2,1,0:T(8,128)(2,1)} %tokens.1) | copy-start | bytes 5898244
  103.5 8.4 %collective-permute-start.1 = (bf16[8,16,8,512]{3,2,1,0:T(8,128)(2,1)S(1)}, bf16[8,16,8,512]{3,2,1,0:T(8,128)(2,1)S(1)}, u32[]{:S(2)}, u32[]{:S(2)}) collective-permute-start(bf16[8,16,8,512]{3,2,1,0:T(8,128)(2,1)S(1)} %all_to_all.50.gm), channel_id=1, source_target_pairs={{0,8},{8,0},{1,9},{9,1},{2,10},{10,2},{3,11},{11,3},{4,12},{12,4},... | collective-permute-start | bytes 3145736 | tf_op jit(solution)/shard_map/ppermute | solution.py:361
  114.7 1.7 %collective-permute-start.2 = (bf16[16,8,640]{2,1,0:T(8,128)(2,1)S(1)}, bf16[16,8,640]{2,1,0:T(8,128)(2,1)S(1)}, u32[]{:S(2)}, u32[]{:S(2)}) collective-permute-start(bf16[16,8,640]{2,1,0:T(8,128)(2,1)S(1)} %get-tuple-element.27), channel_id=1, source_target_pairs={{0,8},{8,0},{1,9},{9,1},{2,10},{10,2},{3,11},{11,3},{4,12},{12,4},... | collective-permute-start | bytes 491528 | tf_op jit(solution)/shard_map/ppermute | solution.py:361
  146.0 6.6 %collective-permute-start.3 = (bf16[16,8,640]{2,1,0:T(8,128)(2,1)S(1)}, bf16[16,8,640]{2,1,0:T(8,128)(2,1)S(1)}, u32[]{:S(2)}, u32[]{:S(2)}) collective-permute-start(bf16[16,8,640]{2,1,0:T(8,128)(2,1)S(1)} %all_to_all.53.mine), channel_id=1, source_target_pairs={{0,8},{8,0},{1,9},{9,1},{2,10},{10,2},{3,11},{11,3},{4,12},{12,4},... | collective-permute-start | bytes 491528 | tf_op jit(solution)/shard_map/ppermute | solution.py:361

commit v3 on v2

--- a/solution.py
+++ b/solution.py
@@ -9,7 +9,6 @@
 
 SIZES = {"yl": 2, "z": 8, "core": 2, "yh": 2, "x": 4}
 AXES = tuple(SIZES)
-OWNERS = ("yl", "z")
 EXP = ("yh", "x")
 PLANE = ("yl", "yh", "x")
 
@@ -208,16 +207,18 @@
     columns, stats = merge_stats([x[0, :, :, 384:].astype(f32).reshape(128, 128) for x in (a_ref, b_ref)])
     for j in range(8):
         wide = [x[j].astype(f32).reshape(128, PART) for x in (a_ref, b_ref)]
-        out[j] = merge_tiles(wide, columns, stats).astype(bf16).reshape(16, 8, PART)
+        merged = merge_tiles(wide, columns, stats).astype(bf16)
+        out[j] = merged[:64].reshape(8, 8, PART)
+        out[8 + j] = merged[64:].reshape(8, 8, PART)
 
 
 def members_body(x_ref, out):
-    blocks = [x_ref[e].astype(f32).reshape(128, PART) for e in range(8)]
-    out[...] = merge_blocks(blocks).reshape(16, 8, PART)
+    blocks = [x_ref[e].astype(f32).reshape(64, PART) for e in range(16)]
+    out[...] = merge_blocks(blocks).reshape(8, 8, PART)
 
 
 def owner_body(x_ref, out, own):
-    merged = merge_blocks([x_ref[d] for d in range(16)])
+    merged = merge_blocks([x_ref[z] for z in range(8)])
     last = merged[:, 384:]
     joined = join_triple(last)
     grad = is_grad_row((8, 1))
@@ -280,19 +281,25 @@
     stats = spread_triple(jnp.where(lane < STAT, 0.0, jnp.where(grad, dots, kept)))
     last = jnp.where(lane < STAT, low[:, 384:], stats)
     full = jnp.concatenate([low[:, :384], last], axis=1).astype(bf16)
-    for d in range(16):
-        out[d] = full
+    for z in range(8):
+        out[z] = full
 
 
 def copies_body(x_ref, out):
-    for e in range(8):
+    for e in range(16):
         out[e] = x_ref[...]
 
 
 def logit_body(tokens, cot, lt_ref, gm, gt, r_mine, r_theirs, dl_ref, w_ref, g_ref, r_sum):
     grad = is_grad_row((256, TOK))
     grad_half = is_grad_row((256, 640))
-    halves = [[g[j].astype(f32).reshape(128, PART) for j in range(8)] for g in (gm, gt)]
+    halves = [
+        [
+            jnp.concatenate([g[8 * yl + j].astype(f32).reshape(64, PART) for yl in range(2)], axis=0)
+            for j in range(8)
+        ]
+        for g in (gm, gt)
+    ]
     dots = [functools.reduce(jnp.add, [part[:, 384:] for part in h]) for h in halves]
     dots = join_triple(jnp.concatenate(dots, axis=0))
     stats = join_triple(jnp.concatenate([h[0][:, 384:] for h in halves], axis=0))
@@ -326,9 +333,31 @@
     r_theirs[...] = r_sum[128:].astype(bf16).reshape(16, 8, 640)
 
 
-def tokens_body(dl_ref, w_ref, rt_ref, g_ref, out):
-    for c in range(CLIPS):
-        out[c] = (dot(dl_ref[c], rt_ref[...], TN) + dot(w_ref[c], g_ref[c], TN)).astype(bf16)
+def tokens_body(clips, dl_ref, w_ref, rt_ref, g_ref, *rest):
+    out, buffer, sems = rest[-3:]
+    copies = []
+    for c in clips:
+        tile = dot(dl_ref[c], rt_ref[...], TN) + dot(w_ref[c], g_ref[c], TN)
+        buffer[c] = tile.astype(bf16)
+        copies.append(pltpu.make_async_copy(buffer.at[c], out.at[c], sems.at[c]))
+        copies[-1].start()
+    for copy in copies:
+        copy.wait()
+
+
+def token_clips(clips, *args):
+    local = (CLIPS, TOK, D)
+    return pl.pallas_call(
+        functools.partial(tokens_body, clips),
+        out_shape=jax.ShapeDtypeStruct(local, bf16),
+        in_specs=[pl.BlockSpec(memory_space=pltpu.VMEM)] * 4
+        + [pl.BlockSpec(memory_space=pltpu.HBM)] * (len(args) - 4),
+        out_specs=pl.BlockSpec(memory_space=pltpu.HBM),
+        scratch_shapes=[pltpu.VMEM(local, bf16), pltpu.SemaphoreType.DMA((CLIPS,))],
+        input_output_aliases={4: 0} if len(args) > 4 else {},
+        compiler_params=pltpu.CompilerParams(vmem_limit_bytes=16 * MiB),
+        cost_estimate=pl.CostEstimate(flops=10**9, bytes_accessed=3 * 10**6, transcendentals=0),
+    )(*args)
 
 
 def add_body(a_ref, b_ref, out):
@@ -364,6 +393,7 @@
 def per_device(tokens, router, w_in, w_out, cotangent):
     core = lax.axis_index("core").astype(jnp.int32).reshape(1)
     values = ((8, 16, 8, PART), bf16)
+    planes = ((16, 8, 8, PART), bf16)
     local = (CLIPS, TOK, D)
     square = ((CLIPS, 256, TOK), bf16)
     mine, theirs, rt, lt = call(
@@ -386,14 +416,14 @@
         nbytes=8 * 10**6,
         limit=24,
     )
-    (sums,) = call(pair_body, [values], mine, to_partner(theirs), flops=10**10, nbytes=3 * 10**6)
+    (sums,) = call(pair_body, [planes], mine, to_partner(theirs), flops=10**10, nbytes=3 * 10**6)
     (sums,) = call(
-        members_body, [((16, 8, PART), f32)], exchange(sums, EXP), flops=10**10, nbytes=10**6
+        members_body, [((8, 8, PART), f32)], exchange(sums, PLANE), flops=10**10, nbytes=10**6
     )
     sums, own = call(
         owner_body,
         [((8, 8, PART), bf16), ((8, PART), f32)],
-        exchange(sums, OWNERS),
+        exchange(sums, ("z",)),
         nbytes=10**5,
     )
     parts, stats = call(
@@ -406,10 +436,10 @@
         nbytes=8 * 10**6,
     )
     (result,) = call(
-        result_body, [((16, 8, PART), bf16)], exchange(parts, EXP), stats, own, nbytes=10**5
-    )
-    (result,) = call(copies_body, [values], exchange(result, OWNERS), nbytes=10**6)
-    g_mine = exchange(result, EXP)
+        result_body, [((8, 8, PART), bf16)], exchange(parts, EXP), stats, own, nbytes=10**5
+    )
+    (result,) = call(copies_body, [planes], exchange(result, ("z",)), nbytes=10**6)
+    g_mine = exchange(result, PLANE)
     g_theirs = to_partner(g_mine)
     half = ((16, 8, 640), bf16)
     r_mine, r_theirs, d_logit, dispatch, grads = call(
@@ -425,10 +455,10 @@
         nbytes=10**7,
         limit=24,
     )
-    (r_mine,) = call(add_body, [half], r_mine, to_partner(r_theirs), nbytes=10**6)
-    (d_tokens,) = call(
-        tokens_body, [(local, bf16)], d_logit, dispatch, rt, grads, flops=10**9, nbytes=6 * 10**6
-    )
+    work = (d_logit, dispatch, rt, grads)
+    got, d_tokens = lax.optimization_barrier((to_partner(r_theirs), token_clips((0,), *work)))
+    (r_mine,) = call(add_body, [half], r_mine, got, nbytes=10**6)
+    d_tokens = token_clips((1, 2), *work, d_tokens)
     r_mine = exchange(r_mine, PLANE)
     (r_mine,) = call(spread_body, [((8, 8, 640), bf16)], r_mine, nbytes=10**5)
     r_mine = exchange(r_mine, ("z",))

time: 154 us -> 150 us (0.974)
  blocking collectives: 115 us -> 110 us
    all_to_all x9, blocking collectives: 115 us -> 110 us  [exchange(): return lax.all_to_all(x, axes, 0, 0, tiled=True)]
    pallas_call x0 -> x2, Pallas kernels: none -> 3.12 us  [token_clips(): pl.pallas_call(functools.partial(tokens_body, clips), out_shape=jax.Shape...]
    pallas_call x13 -> x12, Pallas kernels: 18.7 us -> 16.2 us  [call(): pl.pallas_call(body, out_shape=[jax.ShapeDtypeStruct(s, t) for s, t in ou...]
  transfers between devices with their start and end apart: 4 -> 4, of which waited for: 3 -> 2; matrix products, arithmetic and copies ran while one was open for 0% -> 0% of each run, Pallas kernels for 2% -> 2%
where the time goes in v3:
time: 150 us
  blocking collectives  110 us (73%)
  Pallas kernels  19.3 us (13%)
  starting transfers between devices  15 us (10%)
  waiting for transfers between devices  4.58 us (3%)
    all_to_all x9, blocking collectives, exchange(): return lax.all_to_all(x, axes, 0, 0, tiled=True)  110 us
    pallas_call x12, Pallas kernels, call(): pl.pallas_call(body, out_shape=[jax.ShapeDtypeStruct(s, t) for s, t in ou...  16.2 us
    ppermute x4, starting transfers between devices, to_partner(): return lax.ppermute(x, 'core', [(0, 1), (1, 0)])  15 us
    ppermute x4, waiting for transfers between devices, to_partner(): return lax.ppermute(x, 'core', [(0, 1), (1, 0)])  4.58 us
    pallas_call x2, Pallas kernels, token_clips(): pl.pallas_call(functools.partial(tokens_body, clips), out_shape=jax.Shape...  3.12 us
  transfers between devices with their start and end apart: 4, of which 2 were waited for; matrix products, arithmetic and copies ran while one was open for 0% of the time, Pallas kernels for 2%

profile of v3, /device:TPU:1, one launch (start us, length us, event | category | flops | bytes accessed | tf_op | source)
XLA Modules:
  0.0 149.8 jit_solution(12894242441418798627)
XLA Ops:
  0.6 6.7 %shard_map.68 = (f32[8,16,8,512]{3,2,1,0:T(8,128)S(1)}, bf16[8,16,8,512]{3,2,1,0:T(8,128)(2,1)S(1)}, bf16[256,1280]{1,0:T(8,128)(2,1)S(1)}, f32[3,256,256]{2,1,0:T(8,128)S(1)}) custom-call(s32[1]{0:T(128)} %bitcast.core_ref, bf16[1280,128]{1,0:T(8,128)(2,1)} %router_hbm.1, bf16[3,256,1280]{2,1,0:T(8,128)(2,1)} %tokens.1, bf16[3,256,1280]{2,1,0:T(8,128)(2,1)} %cot.1), custom_call_target="tpu_custom_call" | custom-call | flops 3000000000 | bytes 8000000 | tf_op jit(solution)/shard_map/pallas_call | solution.py:133
  7.4 3.3 %collective-permute-start = (bf16[8,16,8,512]{3,2,1,0:T(8,128)(2,1)S(1)}, bf16[8,16,8,512]{3,2,1,0:T(8,128)(2,1)S(1)}, u32[]{:S(2)}, u32[]{:S(2)}) collective-permute-start(bf16[8,16,8,512]{3,2,1,0:T(8,128)(2,1)S(1)} %get-tuple-element.19), channel_id=1, source_target_pairs={{0,8},{8,0},{1,9},{9,1},{2,10},{10,2},{3,11},{11,3},{4,12},{12,4},... | collective-permute-start | bytes 3145736 | tf_op jit(solution)/shard_map/ppermute | solution.py:390
  10.7 2.3 %collective-permute-done.b_ref = bf16[8,16,8,512]{3,2,1,0:T(8,128)(2,1)S(1)} collective-permute-done((bf16[8,16,8,512]{3,2,1,0:T(8,128)(2,1)S(1)}, bf16[8,16,8,512]{3,2,1,0:T(8,128)(2,1)S(1)}, u32[]{:S(2)}, u32[]{:S(2)}) %collective-permute-start) | collective-permute-done | bytes 1048608 | tf_op jit(solution)/shard_map/ppermute | solution.py:390
  13.0 0.7 shard_map.69
  13.7 21.4 %all_to_all.45.x_ref = bf16[16,8,8,512]{3,2,1,0:T(8,128)(2,1)S(1)} all-to-all(bf16[16,8,8,512]{3,2,1,0:T(8,128)(2,1)S(1)} %shard_map.69), channel_id=1, replica_groups=mesh['yl'=2,'z'=8,'core'=2,'yh'=2,'x'=4] {'yl','yh','x'}, dimensions={0} | all-to-all | bytes 2097152 | tf_op jit(solution)/shard_map/all_to_all | solution.py:386
  35.2 0.0 copy-start
  35.2 0.0 copy-start.1
  35.2 1.0 shard_map.70
  36.2 16.2 %all_to_all.46.x_ref = f32[8,8,512]{2,1,0:T(8,128)S(1)} all-to-all(f32[8,8,512]{2,1,0:T(8,128)S(1)} %shard_map.70), channel_id=1, replica_groups=mesh['yl'=2,'z'=8,'core'=2,'yh'=2,'x'=4] {'z'}, dimensions={0} | all-to-all | bytes 262144 | tf_op jit(solution)/shard_map/all_to_all | solution.py:386
  52.3 0.4 shard_map.71
  52.7 9.1 %all_to_all.47.x_ref = bf16[8,8,512]{2,1,0:T(8,128)(2,1)S(1)} all-to-all(bf16[8,8,512]{2,1,0:T(8,128)(2,1)S(1)} %get-tuple-element.20), channel_id=1, replica_groups=mesh['yl'=2,'z'=8,'core'=2,'yh'=2,'x'=4] {'yh','x'}, dimensions={0} | all-to-all | bytes 131072 | tf_op jit(solution)/shard_map/all_to_all | solution.py:386
  61.8 0.0 copy-done
  61.8 0.0 copy-done.1
  61.8 0.0 copy-start.3
  61.8 3.1 %shard_map.72 = (f32[8,8,512]{2,1,0:T(8,128)S(1)}, f32[8,128]{1,0:T(8,128)S(1)}) custom-call(bf16[8,8,512]{2,1,0:T(8,128)(2,1)S(1)} %all_to_all.47.x_ref, bf16[2,1280,640]{2,1,0:T(8,128)(2,1)S(1)} %copy-done, bf16[2,640,1280]{2,1,0:T(8,128)(2,1)S(1)} %copy-done.1), custom_call_target="tpu_custom_call" | custom-call | flops 1000000000 | bytes 8000000 | tf_op jit(solution)/shard_map/pallas_call | solution.py:133
  64.9 0.0 copy-start.2
  64.9 9.5 %all_to_all.48.x_ref = f32[8,8,512]{2,1,0:T(8,128)S(1)} all-to-all(f32[8,8,512]{2,1,0:T(8,128)S(1)} %get-tuple-element.21), channel_id=1, replica_groups=mesh['yl'=2,'z'=8,'core'=2,'yh'=2,'x'=4] {'yh','x'}, dimensions={0} | all-to-all | bytes 262144 | tf_op jit(solution)/shard_map/all_to_all | solution.py:386
  74.4 0.2 shard_map.73
  74.5 9.6 %all_to_all.49.x_ref = bf16[8,8,512]{2,1,0:T(8,128)(2,1)S(1)} all-to-all(bf16[8,8,512]{2,1,0:T(8,128)(2,1)S(1)} %shard_map.73), channel_id=1, replica_groups=mesh['yl'=2,'z'=8,'core'=2,'yh'=2,'x'=4] {'z'}, dimensions={0} | all-to-all | bytes 131072 | tf_op jit(solution)/shard_map/all_to_all | solution.py:386
  84.1 0.1 shard_map.74
  84.2 14.8 %all_to_all.50.gm = bf16[16,8,8,512]{3,2,1,0:T(8,128)(2,1)S(1)} all-to-all(bf16[16,8,8,512]{3,2,1,0:T(8,128)(2,1)S(1)} %shard_map.74), channel_id=1, replica_groups=mesh['yl'=2,'z'=8,'core'=2,'yh'=2,'x'=4] {'yl','yh','x'}, dimensions={0} | all-to-all | bytes 2097152 | tf_op jit(solution)/shard_map/all_to_all | solution.py:386
  99.0 7.5 %collective-permute-start.1 = (bf16[16,8,8,512]{3,2,1,0:T(8,128)(2,1)S(1)}, bf16[16,8,8,512]{3,2,1,0:T(8,128)(2,1)S(1)}, u32[]{:S(2)}, u32[]{:S(2)}) collective-permute-start(bf16[16,8,8,512]{3,2,1,0:T(8,128)(2,1)S(1)} %all_to_all.50.gm), channel_id=1, source_target_pairs={{0,8},{8,0},{1,9},{9,1},{2,10},{10,2},{3,11},{11,3},{4,12},{12,4},... | collective-permute-start | bytes 3145736 | tf_op jit(solution)/shard_map/ppermute | solution.py:390
  106.5 2.3 %collective-permute-done.1.gt = bf16[16,8,8,512]{3,2,1,0:T(8,128)(2,1)S(1)} collective-permute-done((bf16[16,8,8,512]{3,2,1,0:T(8,128)(2,1)S(1)}, bf16[16,8,8,512]{3,2,1,0:T(8,128)(2,1)S(1)}, u32[]{:S(2)}, u32[]{:S(2)}) %collective-permute-start.1) | collective-permute-done | bytes 1048608 | tf_op jit(solution)/shard_map/ppermute | solution.py:390
  108.8 0.0 copy-done.3
  108.8 0.0 copy-done.2
  108.8 2.7 %shard_map.75 = (bf16[16,8,640]{2,1,0:T(8,128)(2,1)S(1)}, bf16[16,8,640]{2,1,0:T(8,128)(2,1)S(1)}, bf16[3,256,256]{2,1,0:T(8,128)(2,1)S(1)}, bf16[3,256,256]{2,1,0:T(8,128)(2,1)S(1)}, bf16[3,256,1280]{2,1,0:T(8,128)(2,1)S(1)}) custom-call(bf16[3,256,1280]{2,1,0:T(8,128)(2,1)S(1)} %copy-done.2, bf16[3,256,1280]{2,1,0:T(8,128)(2,1)S(1)} %copy-done.3, ...), custom_call_target="tpu_custom_call" | custom-call | flops 3000000000 | bytes 10000000 | tf_op jit(solution)/shard_map/pallas_call | solution.py:133
  111.5 0.6 collective-permute-start.2
  112.1 1.4 shard_map.76.rest_0_
  113.5 0.0 collective-permute-done.2.b_ref
  113.6 10.2 %all_to_all.51.x_ref = bf16[16,8,640]{2,1,0:T(8,128)(2,1)S(1)} all-to-all(bf16[16,8,640]{2,1,0:T(8,128)(2,1)S(1)} %shard_map.78), channel_id=1, replica_groups=mesh['yl'=2,'z'=8,'core'=2,'yh'=2,'x'=4] {'yl','yh','x'}, dimensions={0} | all-to-all | bytes 327680 | tf_op jit(solution)/shard_map/all_to_all | solution.py:386
  123.8 9.9 %all_to_all.52.x_ref = bf16[8,8,640]{2,1,0:T(8,128)(2,1)S(1)} all-to-all(bf16[8,8,640]{2,1,0:T(8,128)(2,1)S(1)} %shard_map.79), channel_id=1, replica_groups=mesh['yl'=2,'z'=8,'core'=2,'yh'=2,'x'=4] {'z'}, dimensions={0} | all-to-all | bytes 163840 | tf_op jit(solution)/shard_map/all_to_all | solution.py:386
  133.7 9.6 %all_to_all.53.mine = bf16[16,8,640]{2,1,0:T(8,128)(2,1)S(1)} all-to-all(bf16[16,8,640]{2,1,0:T(8,128)(2,1)S(1)} %shard_map.80), channel_id=1, replica_groups=mesh['yl'=2,'z'=8,'core'=2,'yh'=2,'x'=4] {'yl','yh','x'}, dimensions={0} | all-to-all | bytes 327680 | tf_op jit(solution)/shard_map/all_to_all | solution.py:386
  143.3 3.5 %collective-permute-start.3 = (bf16[16,8,640]{2,1,0:T(8,128)(2,1)S(1)}, bf16[16,8,640]{2,1,0:T(8,128)(2,1)S(1)}, u32[]{:S(2)}, u32[]{:S(2)}) collective-permute-start(bf16[16,8,640]{2,1,0:T(8,128)(2,1)S(1)} %all_to_all.53.mine), channel_id=1, source_target_pairs={{0,8},{8,0},{1,9},{9,1},{2,10},{10,2},{3,11},{11,3},{4,12},{12,4},... | collective-permute-start | bytes 491528 | tf_op jit(solution)/shard_map/ppermute | solution.py:390
  146.8 1.7 %shard_map.77 = bf16[3,256,1280]{2,1,0:T(8,128)(2,1)} custom-call(bf16[3,256,256]{2,1,0:T(8,128)(2,1)S(1)} %get-tuple-element.24.dl_ref, bf16[3,256,256]{2,1,0:T(8,128)(2,1)S(1)} %get-tuple-element.25.w_ref, bf16[256,1280]{1,0:T(8,128)(2,1)S(1)} %get-tuple-element.26.rt_ref, ...), custom_call_target="tpu_custom_call", output_to_operand_aliasing={{}: (4, {})} | custom-call | flops 1000000000 | bytes 3000000 | tf_op jit(solution)/shard_map/pallas_call | solution.py:350
  148.6 0.0 collective-permute-done.3.theirs
  148.6 1.3 shard_map.81
  (3 shorter events, 0.1 us)
Async XLA Ops:
  7.4 5.6 %collective-permute-start = (bf16[8,16,8,512]{3,2,1,0:T(8,128)(2,1)S(1)}, bf16[8,16,8,512]{3,2,1,0:T(8,128)(2,1)S(1)}, u32[]{:S(2)}, u32[]{:S(2)}) collective-permute-start(bf16[8,16,8,512]{3,2,1,0:T(8,128)(2,1)S(1)} %get-tuple-element.19), channel_id=1, source_target_pairs={{0,8},{8,0},{1,9},{9,1},{2,10},{10,2},{3,11},{11,3},{4,12},{12,4},... | collective-permute-start | bytes 3145736 | tf_op jit(solution)/shard_map/ppermute | solution.py:390
  35.2 26.6 %copy-start = (bf16[2,1280,640]{2,1,0:T(8,128)(2,1)S(1)}, bf16[2,1280,640]{2,1,0:T(8,128)(2,1)}, u32[]{:S(2)}) copy-start(bf16[2,1280,640]{2,1,0:T(8,128)(2,1)} %w_in.1) | copy-start | bytes 9830404
  35.2 26.6 %copy-start.1 = (bf16[2,640,1280]{2,1,0:T(8,128)(2,1)S(1)}, bf16[2,640,1280]{2,1,0:T(8,128)(2,1)}, u32[]{:S(2)}) copy-start(bf16[2,640,1280]{2,1,0:T(8,128)(2,1)} %w_out.1) | copy-start | bytes 9830404
  61.8 47.0 %copy-start.3 = (bf16[3,256,1280]{2,1,0:T(8,128)(2,1)S(1)}, bf16[3,256,1280]{2,1,0:T(8,128)(2,1)}, u32[]{:S(2)}) copy-start(bf16[3,256,1280]{2,1,0:T(8,128)(2,1)} %cot.1) | copy-start | bytes 5898244
  64.9 43.9 %copy-start.2 = (bf16[3,256,1280]{2,1,0:T(8,128)(2,1)S(1)}, bf16[3,256,1280]{2,1,0:T(8,128)(2,1)}, u32[]{:S(2)}) copy-start(bf16[3,256,1280]{2,1,0:T(8,128)(2,1)} %tokens.1) | copy-start | bytes 5898244
  99.0 9.8 %collective-permute-start.1 = (bf16[16,8,8,512]{3,2,1,0:T(8,128)(2,1)S(1)}, bf16[16,8,8,512]{3,2,1,0:T(8,128)(2,1)S(1)}, u32[]{:S(2)}, u32[]{:S(2)}) collective-permute-start(bf16[16,8,8,512]{3,2,1,0:T(8,128)(2,1)S(1)} %all_to_all.50.gm), channel_id=1, source_target_pairs={{0,8},{8,0},{1,9},{9,1},{2,10},{10,2},{3,11},{11,3},{4,12},{12,4},... | collective-permute-start | bytes 3145736 | tf_op jit(solution)/shard_map/ppermute | solution.py:390
  111.5 2.0 %collective-permute-start.2 = (bf16[16,8,640]{2,1,0:T(8,128)(2,1)S(1)}, bf16[16,8,640]{2,1,0:T(8,128)(2,1)S(1)}, u32[]{:S(2)}, u32[]{:S(2)}) collective-permute-start(bf16[16,8,640]{2,1,0:T(8,128)(2,1)S(1)} %get-tuple-element.28), channel_id=1, source_target_pairs={{0,8},{8,0},{1,9},{9,1},{2,10},{10,2},{3,11},{11,3},{4,12},{12,4},... | collective-permute-start | bytes 491528 | tf_op jit(solution)/shard_map/ppermute | solution.py:390
  143.3 5.3 %collective-permute-start.3 = (bf16[16,8,640]{2,1,0:T(8,128)(2,1)S(1)}, bf16[16,8,640]{2,1,0:T(8,128)(2,1)S(1)}, u32[]{:S(2)}, u32[]{:S(2)}) collective-permute-start(bf16[16,8,640]{2,1,0:T(8,128)(2,1)S(1)} %all_to_all.53.mine), channel_id=1, source_target_pairs={{0,8},{8,0},{1,9},{9,1},{2,10},{10,2},{3,11},{11,3},{4,12},{12,4},... | collective-permute-start | bytes 491528 | tf_op jit(solution)/shard_map/ppermute | solution.py:390

commit v4 on v3

--- a/solution.py
+++ b/solution.py
@@ -149,9 +149,26 @@
     return s == slot, t
 
 
+def fill_parts(out, weights_in, weights_out, tokens, cot, stats, before=None):
+    def product(c, lanes):
+        return dot(weights_in[c], tokens[c, :, lanes]) + dot(weights_out[c], cot[c, :, lanes])
+
+    for c in range(CLIPS):
+        if before is not None:
+            before[c].wait()
+        for i in range(4):
+            part = product(c, slice(256 * i, 256 * i + 256)).reshape(16, 8, 256)
+            for h in range(2):
+                tile = part[:, :, 128 * h : 128 * h + 128]
+                out[2 * i + h, :, :, 128 * c : 128 * c + 128] = tile.astype(out.dtype)
+    tails = [product(c, slice(1024, 1280)) for c in range(CLIPS)]
+    for j in range(8):
+        out[j, :, :, 384:] = last_tile(tails, j, stats).reshape(16, 8, 128).astype(out.dtype)
+
+
 def slots_body(
-    core_ref, router_hbm, tokens_hbm, cot_hbm, mine, theirs, rt_ref, lt_ref,
-    router, tokens, cot, weights_in, weights_out, sems, router_sem,
+    core_ref, router_hbm, tokens_hbm, cot_hbm, theirs, rt_ref, lt_ref, tokens, cot,
+    own_in, own_out, own_stats, router, weights_in, weights_out, sems, router_sem,
 ):
     first = pltpu.make_async_copy(router_hbm, router, router_sem)
     copies = [
@@ -160,47 +177,41 @@
         for c in range(CLIPS)
     ]
     first.start()
-    for copy in copies:
-        copy.start()
+    copies[0].start()
     pick, _ = slot_of_row(core_ref[0])
     pick = pick.astype(f32).astype(bf16)
     first.wait()
+    copies[1].start()
     rt_ref[...] = dot(pick, router[...], NT).astype(bf16)
     grad = is_grad_row((256, TOK))
     lane = lanes_of((256, 128))
     stats = jnp.zeros((256, 128), f32)
     for c in range(CLIPS):
         copies[c].wait()
+        for copy in copies[2 * c + 2 : min(2 * c + 4, 6)]:
+            copy.start()
         logits = dot(rt_ref[...], tokens[c], NT)
         lt_ref[c] = logits
         peak = jnp.max(logits, axis=1, keepdims=True)
         low = jnp.where(grad, 0.0, jnp.exp(logits - peak)).astype(bf16)
         total = jnp.sum(low.astype(f32), axis=1, keepdims=True)
-        weights_in[c] = low
+        own_in[c] = low[:128]
+        weights_in[c] = low[128:]
         raised = jnp.exp(logits - jnp.max(logits, axis=0, keepdims=True))
         combine = raised * (2.0 / jnp.sum(raised, axis=0, keepdims=True))
-        weights_out[c] = jnp.where(grad, combine, 0.0).astype(bf16)
+        combine = jnp.where(grad, combine, 0.0).astype(bf16)
+        own_out[c] = combine[:128]
+        weights_out[c] = combine[128:]
         at = STAT + 8 * c
         stats = jnp.where(lane == at, peak, jnp.where(lane == at + 3, total, stats))
     ones = jnp.where((lane >= STAT) & (lane % 8 == 3), 1.0, 0.0)
     stats = spread_triple(jnp.where(is_grad_row((256, 128)), ones, stats))
-
-    def product(c, lanes):
-        return dot(weights_in[c], tokens[c, :, lanes]) + dot(weights_out[c], cot[c, :, lanes])
-
-    for c in range(CLIPS):
-        copies[CLIPS + c].wait()
-        for i in range(4):
-            part = product(c, slice(256 * i, 256 * i + 256)).reshape(32, 8, 256)
-            for h in range(2):
-                tile = part[:, :, 128 * h : 128 * h + 128]
-                mine[2 * i + h, :, :, 128 * c : 128 * c + 128] = tile[:16]
-                theirs[2 * i + h, :, :, 128 * c : 128 * c + 128] = tile[16:].astype(bf16)
-    tails = [product(c, slice(1024, 1280)) for c in range(CLIPS)]
-    for j in range(8):
-        tile = last_tile(tails, j, stats).reshape(32, 8, 128)
-        mine[j, :, :, 384:] = tile[:16]
-        theirs[j, :, :, 384:] = tile[16:].astype(bf16)
+    own_stats[...] = stats[:128]
+    fill_parts(theirs, weights_in, weights_out, tokens, cot, stats[128:], copies[CLIPS:])
+
+
+def own_body(own_in, own_out, own_stats, tokens, cot, mine):
+    fill_parts(mine, own_in, own_out, tokens, cot, own_stats[...])
 
 
 def pair_body(a_ref, b_ref, out):
@@ -290,23 +301,40 @@
         out[e] = x_ref[...]
 
 
-def logit_body(tokens, cot, lt_ref, gm, gt, r_mine, r_theirs, dl_ref, w_ref, g_ref, r_sum):
+def half_of(g, tokens, cot, low_ref):
+    blocks = [
+        jnp.concatenate([g[8 * yl + j].astype(f32).reshape(64, PART) for yl in range(2)], axis=0)
+        for j in range(8)
+    ]
+    dots = functools.reduce(jnp.add, [part[:, 384:] for part in blocks])
+    d_combine, d_dispatch = [], []
+    for c in range(CLIPS):
+        low = rows_of(blocks, c).astype(bf16)
+        low_ref[c] = low
+        d_combine.append(dot(low, cot[c], NT))
+        d_dispatch.append(dot(low, tokens[c], NT))
+    return d_combine, d_dispatch, join_triple(dots), join_triple(blocks[0][:, 384:])
+
+
+def near_body(tokens, cot, g, low_ref, dc_ref, dd_ref, dots_ref, stats_ref):
+    d_combine, d_dispatch, dots, stats = half_of(g, tokens, cot, low_ref)
+    for c in range(CLIPS):
+        dc_ref[c] = d_combine[c]
+        dd_ref[c] = d_dispatch[c]
+    dots_ref[...] = dots
+    stats_ref[...] = stats
+
+
+def logit_body(
+    tokens, cot, lt_ref, dc_ref, dd_ref, dots_ref, stats_ref, g,
+    r_mine, r_theirs, dl_ref, w_ref, low_ref, r_sum,
+):
     grad = is_grad_row((256, TOK))
     grad_half = is_grad_row((256, 640))
-    halves = [
-        [
-            jnp.concatenate([g[8 * yl + j].astype(f32).reshape(64, PART) for yl in range(2)], axis=0)
-            for j in range(8)
-        ]
-        for g in (gm, gt)
-    ]
-    dots = [functools.reduce(jnp.add, [part[:, 384:] for part in h]) for h in halves]
-    dots = join_triple(jnp.concatenate(dots, axis=0))
-    stats = join_triple(jnp.concatenate([h[0][:, 384:] for h in halves], axis=0))
-    stats = pltpu.roll(stats, 4, 0)
-    for c in range(CLIPS):
-        low = jnp.concatenate([rows_of(h, c).astype(bf16) for h in halves], axis=0)
-        g_ref[c] = low
+    far_combine, far_dispatch, far_dots, far_stats = half_of(g, tokens, cot, low_ref)
+    dots = jnp.concatenate([dots_ref[...], far_dots], axis=0)
+    stats = pltpu.roll(jnp.concatenate([stats_ref[...], far_stats], axis=0), 4, 0)
+    for c in range(CLIPS):
         at = STAT + 8 * c
         peak = stats[:, at : at + 1]
         total = stats[:, at + 3 : at + 4]
@@ -315,10 +343,10 @@
         raised = jnp.exp(logits - jnp.max(logits, axis=0, keepdims=True))
         combine = raised * (2.0 / jnp.sum(raised, axis=0, keepdims=True))
         combine = jnp.where(grad, 0.0, combine)
-        d_combine = dot(low, cot[c], NT)
+        d_combine = jnp.concatenate([dc_ref[c], far_combine[c]], axis=0)
         inner = jnp.sum(combine * d_combine, axis=0, keepdims=True)
         dispatch = jnp.where(grad, jnp.exp(logits - peak) * (1.0 / total), 0.0)
-        d_dispatch = dot(low, tokens[c], NT)
+        d_dispatch = jnp.concatenate([dd_ref[c], far_dispatch[c]], axis=0)
         own = jnp.where(grad, dispatch * (d_dispatch - column_dot), combine * (d_combine - inner))
         d_logit = (own + swap_halves(own, grad)).astype(bf16)
         part = dot(d_logit, tokens[c])
@@ -333,11 +361,12 @@
     r_theirs[...] = r_sum[128:].astype(bf16).reshape(16, 8, 640)
 
 
-def tokens_body(clips, dl_ref, w_ref, rt_ref, g_ref, *rest):
+def tokens_body(clips, dl_ref, w_ref, rt_ref, near_ref, far_ref, *rest):
     out, buffer, sems = rest[-3:]
     copies = []
     for c in clips:
-        tile = dot(dl_ref[c], rt_ref[...], TN) + dot(w_ref[c], g_ref[c], TN)
+        rows = jnp.concatenate([near_ref[c], far_ref[c]], axis=0)
+        tile = dot(dl_ref[c], rt_ref[...], TN) + dot(w_ref[c], rows, TN)
         buffer[c] = tile.astype(bf16)
         copies.append(pltpu.make_async_copy(buffer.at[c], out.at[c], sems.at[c]))
         copies[-1].start()
@@ -350,11 +379,11 @@
     return pl.pallas_call(
         functools.partial(tokens_body, clips),
         out_shape=jax.ShapeDtypeStruct(local, bf16),
-        in_specs=[pl.BlockSpec(memory_space=pltpu.VMEM)] * 4
-        + [pl.BlockSpec(memory_space=pltpu.HBM)] * (len(args) - 4),
+        in_specs=[pl.BlockSpec(memory_space=pltpu.VMEM)] * 5
+        + [pl.BlockSpec(memory_space=pltpu.HBM)] * (len(args) - 5),
         out_specs=pl.BlockSpec(memory_space=pltpu.HBM),
         scratch_shapes=[pltpu.VMEM(local, bf16), pltpu.SemaphoreType.DMA((CLIPS,))],
-        input_output_aliases={4: 0} if len(args) > 4 else {},
+        input_output_aliases={5: 0} if len(args) > 5 else {},
         compiler_params=pltpu.CompilerParams(vmem_limit_bytes=16 * MiB),
         cost_estimate=pl.CostEstimate(flops=10**9, bytes_accessed=3 * 10**6, transcendentals=0),
     )(*args)
@@ -396,17 +425,25 @@
     planes = ((16, 8, 8, PART), bf16)
     local = (CLIPS, TOK, D)
     square = ((CLIPS, 256, TOK), bf16)
-    mine, theirs, rt, lt = call(
+    own = ((CLIPS, 128, TOK), bf16)
+    theirs, rt, lt, tokens, cotangent, own_in, own_out, own_stats = call(
         slots_body,
-        [(values[0], f32), values, ((256, D), bf16), ((CLIPS, 256, TOK), f32)],
+        [
+            values,
+            ((256, D), bf16),
+            ((CLIPS, 256, TOK), f32),
+            (local, bf16),
+            (local, bf16),
+            own,
+            own,
+            ((128, 128), f32),
+        ],
         core,
         *[pltpu.with_memory_space_constraint(x, pltpu.HBM) for x in (router, tokens, cotangent)],
         scratch=[
             pltpu.VMEM((D, 128), bf16),
-            pltpu.VMEM(local, bf16),
-            pltpu.VMEM(local, bf16),
-            pltpu.VMEM(*square),
-            pltpu.VMEM(*square),
+            pltpu.VMEM(*own),
+            pltpu.VMEM(*own),
             pltpu.SemaphoreType.DMA((2, CLIPS)),
             pltpu.SemaphoreType.DMA,
         ],
@@ -416,6 +453,18 @@
         nbytes=8 * 10**6,
         limit=24,
     )
+    (mine,) = call(
+        own_body,
+        [(values[0], f32)],
+        own_in,
+        own_out,
+        own_stats,
+        tokens,
+        cotangent,
+        flops=10**9,
+        nbytes=8 * 10**6,
+        limit=24,
+    )
     (sums,) = call(pair_body, [planes], mine, to_partner(theirs), flops=10**10, nbytes=3 * 10**6)
     (sums,) = call(
         members_body, [((8, 8, PART), f32)], exchange(sums, PLANE), flops=10**10, nbytes=10**6
@@ -442,20 +491,33 @@
     g_mine = exchange(result, PLANE)
     g_theirs = to_partner(g_mine)
     half = ((16, 8, 640), bf16)
-    r_mine, r_theirs, d_logit, dispatch, grads = call(
+    pair = ((CLIPS, 128, TOK), f32)
+    near, d_combine, d_dispatch, dots, stats = call(
+        near_body,
+        [((CLIPS, 128, D), bf16), pair, pair, ((128, 128), f32), ((128, 128), f32)],
+        tokens,
+        cotangent,
+        g_mine,
+        flops=10**9,
+        nbytes=6 * 10**6,
+    )
+    r_mine, r_theirs, d_logit, dispatch, far = call(
         logit_body,
-        [half, half, square, square, (local, bf16)],
+        [half, half, square, square, ((CLIPS, 128, D), bf16)],
         tokens,
         cotangent,
         lt,
-        g_mine,
+        d_combine,
+        d_dispatch,
+        dots,
+        stats,
         g_theirs,
         scratch=[pltpu.VMEM((256, 640), f32)],
         flops=3 * 10**9,
         nbytes=10**7,
         limit=24,
     )
-    work = (d_logit, dispatch, rt, grads)
+    work = (d_logit, dispatch, rt, near, far)
     got, d_tokens = lax.optimization_barrier((to_partner(r_theirs), token_clips((0,), *work)))
     (r_mine,) = call(add_body, [half], r_mine, got, nbytes=10**6)
     d_tokens = token_clips((1, 2), *work, d_tokens)

time: 150 us -> 148 us (0.987)
  waiting for transfers between devices: 4.58 us -> 2.12 us
    ppermute x4, waiting for transfers between devices: 4.58 us -> 2.12 us  [to_partner(): return lax.ppermute(x, 'core', [(0, 1), (1, 0)])]
    pallas_call x12 -> x14, Pallas kernels: 16.2 us -> 16.6 us  [call(): pl.pallas_call(body, out_shape=[jax.ShapeDtypeStruct(s, t) for s, t in ou...]
  transfers between devices with their start and end apart: 4 -> 4, of which waited for: 2 -> 2; matrix products, arithmetic and copies ran while one was open for 0% -> 0% of each run, Pallas kernels for 2% -> 4%
where the time goes in v4:
time: 148 us; the launch traced here: 147 us
  blocking collectives  110 us (74%)
  Pallas kernels  19.7 us (13%)
  starting transfers between devices  14.8 us (10%)
  waiting for transfers between devices  2.12 us (1%)
    all_to_all x9, blocking collectives, exchange(): return lax.all_to_all(x, axes, 0, 0, tiled=True)  110 us
    pallas_call x14, Pallas kernels, call(): pl.pallas_call(body, out_shape=[jax.ShapeDtypeStruct(s, t) for s, t in ou...  16.6 us
    ppermute x4, starting transfers between devices, to_partner(): return lax.ppermute(x, 'core', [(0, 1), (1, 0)])  14.8 us
    pallas_call x2, Pallas kernels, token_clips(): pl.pallas_call(functools.partial(tokens_body, clips), out_shape=jax.Shape...  3.12 us
  transfers between devices with their start and end apart: 4, of which 2 were waited for; matrix products, arithmetic and copies ran while one was open for 0% of the time, Pallas kernels for 4%

profile of v4, /device:TPU:1, one launch (start us, length us, event | category | flops | bytes accessed | tf_op | source)
XLA Modules:
  0.0 147.5 jit_solution(8713235736804526974)
XLA Ops:
  0.6 5.0 %shard_map.68 = (bf16[8,16,8,512]{3,2,1,0:T(8,128)(2,1)S(1)}, bf16[256,1280]{1,0:T(8,128)(2,1)S(1)}, f32[3,256,256]{2,1,0:T(8,128)S(1)}, bf16[3,256,1280]{2,1,0:...) custom-call(s32[1]{0:T(128)} %bitcast.core_ref, ...), custom_call_target="tpu_custom_call" | custom-call | flops 3000000000 | bytes 8000000 | tf_op jit(solution)/shard_map/pallas_call | solution.py:133
  5.6 3.3 %collective-permute-start = (bf16[8,16,8,512]{3,2,1,0:T(8,128)(2,1)S(1)}, bf16[8,16,8,512]{3,2,1,0:T(8,128)(2,1)S(1)}, u32[]{:S(2)}, u32[]{:S(2)}) collective-permute-start(bf16[8,16,8,512]{3,2,1,0:T(8,128)(2,1)S(1)} %get-tuple-element.32), channel_id=1, source_target_pairs={{0,8},{8,0},{1,9},{9,1},{2,10},{10,2},{3,11},{11,3},{4,12},{12,4},... | collective-permute-start | bytes 3145736 | tf_op jit(solution)/shard_map/ppermute | solution.py:419
  9.0 1.0 shard_map.69.a_ref
  10.0 1.3 collective-permute-done.b_ref
  11.3 0.7 shard_map.70
  12.0 21.4 %all_to_all.45.x_ref = bf16[16,8,8,512]{3,2,1,0:T(8,128)(2,1)S(1)} all-to-all(bf16[16,8,8,512]{3,2,1,0:T(8,128)(2,1)S(1)} %shard_map.70), channel_id=1, replica_groups=mesh['yl'=2,'z'=8,'core'=2,'yh'=2,'x'=4] {'yl','yh','x'}, dimensions={0} | all-to-all | bytes 2097152 | tf_op jit(solution)/shard_map/all_to_all | solution.py:415
  33.5 0.0 copy-start
  33.5 0.0 copy-start.1
  33.5 1.0 shard_map.71
  34.4 16.2 %all_to_all.46.x_ref = f32[8,8,512]{2,1,0:T(8,128)S(1)} all-to-all(f32[8,8,512]{2,1,0:T(8,128)S(1)} %shard_map.71), channel_id=1, replica_groups=mesh['yl'=2,'z'=8,'core'=2,'yh'=2,'x'=4] {'z'}, dimensions={0} | all-to-all | bytes 262144 | tf_op jit(solution)/shard_map/all_to_all | solution.py:415
  50.6 0.4 shard_map.72
  51.0 9.1 %all_to_all.47.x_ref = bf16[8,8,512]{2,1,0:T(8,128)(2,1)S(1)} all-to-all(bf16[8,8,512]{2,1,0:T(8,128)(2,1)S(1)} %get-tuple-element.33), channel_id=1, replica_groups=mesh['yl'=2,'z'=8,'core'=2,'yh'=2,'x'=4] {'yh','x'}, dimensions={0} | all-to-all | bytes 131072 | tf_op jit(solution)/shard_map/all_to_all | solution.py:415
  60.1 0.0 copy-done
  60.1 0.0 copy-done.1
  60.1 3.1 %shard_map.73 = (f32[8,8,512]{2,1,0:T(8,128)S(1)}, f32[8,128]{1,0:T(8,128)S(1)}) custom-call(bf16[8,8,512]{2,1,0:T(8,128)(2,1)S(1)} %all_to_all.47.x_ref, bf16[2,1280,640]{2,1,0:T(8,128)(2,1)S(1)} %copy-done, bf16[2,640,1280]{2,1,0:T(8,128)(2,1)S(1)} %copy-done.1), custom_call_target="tpu_custom_call" | custom-call | flops 1000000000 | bytes 8000000 | tf_op jit(solution)/shard_map/pallas_call | solution.py:133
  63.2 9.3 %all_to_all.48.x_ref = f32[8,8,512]{2,1,0:T(8,128)S(1)} all-to-all(f32[8,8,512]{2,1,0:T(8,128)S(1)} %get-tuple-element.34), channel_id=1, replica_groups=mesh['yl'=2,'z'=8,'core'=2,'yh'=2,'x'=4] {'yh','x'}, dimensions={0} | all-to-all | bytes 262144 | tf_op jit(solution)/shard_map/all_to_all | solution.py:415
  72.5 0.2 shard_map.74
  72.7 9.6 %all_to_all.49.x_ref = bf16[8,8,512]{2,1,0:T(8,128)(2,1)S(1)} all-to-all(bf16[8,8,512]{2,1,0:T(8,128)(2,1)S(1)} %shard_map.74), channel_id=1, replica_groups=mesh['yl'=2,'z'=8,'core'=2,'yh'=2,'x'=4] {'z'}, dimensions={0} | all-to-all | bytes 131072 | tf_op jit(solution)/shard_map/all_to_all | solution.py:415
  82.3 0.1 shard_map.75
  82.3 14.8 %all_to_all.50.g = bf16[16,8,8,512]{3,2,1,0:T(8,128)(2,1)S(1)} all-to-all(bf16[16,8,8,512]{3,2,1,0:T(8,128)(2,1)S(1)} %shard_map.75), channel_id=1, replica_groups=mesh['yl'=2,'z'=8,'core'=2,'yh'=2,'x'=4] {'yl','yh','x'}, dimensions={0} | all-to-all | bytes 2097152 | tf_op jit(solution)/shard_map/all_to_all | solution.py:415
  97.1 7.5 %collective-permute-start.1 = (bf16[16,8,8,512]{3,2,1,0:T(8,128)(2,1)S(1)}, bf16[16,8,8,512]{3,2,1,0:T(8,128)(2,1)S(1)}, u32[]{:S(2)}, u32[]{:S(2)}) collective-permute-start(bf16[16,8,8,512]{3,2,1,0:T(8,128)(2,1)S(1)} %all_to_all.50.g), channel_id=1, source_target_pairs={{0,8},{8,0},{1,9},{9,1},{2,10},{10,2},{3,11},{11,3},{4,12},{12,4},... | collective-permute-start | bytes 3145736 | tf_op jit(solution)/shard_map/ppermute | solution.py:419
  104.6 1.4 shard_map.76
  106.0 0.9 collective-permute-done.1.g
  106.9 2.4 %shard_map.77 = (bf16[16,8,640]{2,1,0:T(8,128)(2,1)S(1)}, bf16[16,8,640]{2,1,0:T(8,128)(2,1)S(1)}, bf16[3,256,256]{2,1,0:T(8,128)(2,1)S(1)}, bf16[3,256,256]{2,1,0:T(8,128)(2,1)S(1)}, bf16[3,128,1280]{2,1,0:T(8,128)(2,1)S(1)}) custom-call(bf16[3,256,1280]{2,1,0:T(8,128)(2,1)S(1)} %get-tuple-element.26.tokens, ...), custom_call_target="tpu_custom_call" | custom-call | flops 3000000000 | bytes 10000000 | tf_op jit(solution)/shard_map/pallas_call | solution.py:133
  109.3 0.5 collective-permute-start.2
  109.7 1.4 shard_map.78.rest_0_
  111.1 0.0 collective-permute-done.2.b_ref
  111.2 10.2 %all_to_all.51.x_ref = bf16[16,8,640]{2,1,0:T(8,128)(2,1)S(1)} all-to-all(bf16[16,8,640]{2,1,0:T(8,128)(2,1)S(1)} %shard_map.80), channel_id=1, replica_groups=mesh['yl'=2,'z'=8,'core'=2,'yh'=2,'x'=4] {'yl','yh','x'}, dimensions={0} | all-to-all | bytes 327680 | tf_op jit(solution)/shard_map/all_to_all | solution.py:415
  121.4 9.9 %all_to_all.52.x_ref = bf16[8,8,640]{2,1,0:T(8,128)(2,1)S(1)} all-to-all(bf16[8,8,640]{2,1,0:T(8,128)(2,1)S(1)} %shard_map.81), channel_id=1, replica_groups=mesh['yl'=2,'z'=8,'core'=2,'yh'=2,'x'=4] {'z'}, dimensions={0} | all-to-all | bytes 163840 | tf_op jit(solution)/shard_map/all_to_all | solution.py:415
  131.3 9.6 %all_to_all.53.mine = bf16[16,8,640]{2,1,0:T(8,128)(2,1)S(1)} all-to-all(bf16[16,8,640]{2,1,0:T(8,128)(2,1)S(1)} %shard_map.82), channel_id=1, replica_groups=mesh['yl'=2,'z'=8,'core'=2,'yh'=2,'x'=4] {'yl','yh','x'}, dimensions={0} | all-to-all | bytes 327680 | tf_op jit(solution)/shard_map/all_to_all | solution.py:415
  140.9 3.5 %collective-permute-start.3 = (bf16[16,8,640]{2,1,0:T(8,128)(2,1)S(1)}, bf16[16,8,640]{2,1,0:T(8,128)(2,1)S(1)}, u32[]{:S(2)}, u32[]{:S(2)}) collective-permute-start(bf16[16,8,640]{2,1,0:T(8,128)(2,1)S(1)} %all_to_all.53.mine), channel_id=1, source_target_pairs={{0,8},{8,0},{1,9},{9,1},{2,10},{10,2},{3,11},{11,3},{4,12},{12,4},... | collective-permute-start | bytes 491528 | tf_op jit(solution)/shard_map/ppermute | solution.py:419
  144.4 1.7 %shard_map.79 = bf16[3,256,1280]{2,1,0:T(8,128)(2,1)} custom-call(bf16[3,256,256]{2,1,0:T(8,128)(2,1)S(1)} %get-tuple-element.41.dl_ref, bf16[3,256,256]{2,1,0:T(8,128)(2,1)S(1)} %get-tuple-element.42.w_ref, bf16[256,1280]{1,0:T(8,128)(2,1)S(1)} %get-tuple-element.43.rt_ref, ...), custom_call_target="tpu_custom_call", output_to_operand_aliasing={{}: (5, {})} | custom-call | flops 1000000000 | bytes 3000000 | tf_op jit(solution)/shard_map/pallas_call | solution.py:379
  146.2 0.0 collective-permute-done.3.theirs
  146.2 1.3 shard_map.83
  (3 shorter events, 0.1 us)
Async XLA Ops:
  5.6 5.6 %collective-permute-start = (bf16[8,16,8,512]{3,2,1,0:T(8,128)(2,1)S(1)}, bf16[8,16,8,512]{3,2,1,0:T(8,128)(2,1)S(1)}, u32[]{:S(2)}, u32[]{:S(2)}) collective-permute-start(bf16[8,16,8,512]{3,2,1,0:T(8,128)(2,1)S(1)} %get-tuple-element.32), channel_id=1, source_target_pairs={{0,8},{8,0},{1,9},{9,1},{2,10},{10,2},{3,11},{11,3},{4,12},{12,4},... | collective-permute-start | bytes 3145736 | tf_op jit(solution)/shard_map/ppermute | solution.py:419
  33.5 26.6 %copy-start = (bf16[2,1280,640]{2,1,0:T(8,128)(2,1)S(1)}, bf16[2,1280,640]{2,1,0:T(8,128)(2,1)}, u32[]{:S(2)}) copy-start(bf16[2,1280,640]{2,1,0:T(8,128)(2,1)} %w_in.1) | copy-start | bytes 9830404
  33.5 26.6 %copy-start.1 = (bf16[2,640,1280]{2,1,0:T(8,128)(2,1)S(1)}, bf16[2,640,1280]{2,1,0:T(8,128)(2,1)}, u32[]{:S(2)}) copy-start(bf16[2,640,1280]{2,1,0:T(8,128)(2,1)} %w_out.1) | copy-start | bytes 9830404
  97.1 9.8 %collective-permute-start.1 = (bf16[16,8,8,512]{3,2,1,0:T(8,128)(2,1)S(1)}, bf16[16,8,8,512]{3,2,1,0:T(8,128)(2,1)S(1)}, u32[]{:S(2)}, u32[]{:S(2)}) collective-permute-start(bf16[16,8,8,512]{3,2,1,0:T(8,128)(2,1)S(1)} %all_to_all.50.g), channel_id=1, source_target_pairs={{0,8},{8,0},{1,9},{9,1},{2,10},{10,2},{3,11},{11,3},{4,12},{12,4},... | collective-permute-start | bytes 3145736 | tf_op jit(solution)/shard_map/ppermute | solution.py:419
  109.3 1.9 %collective-permute-start.2 = (bf16[16,8,640]{2,1,0:T(8,128)(2,1)S(1)}, bf16[16,8,640]{2,1,0:T(8,128)(2,1)S(1)}, u32[]{:S(2)}, u32[]{:S(2)}) collective-permute-start(bf16[16,8,640]{2,1,0:T(8,128)(2,1)S(1)} %get-tuple-element.46), channel_id=1, source_target_pairs={{0,8},{8,0},{1,9},{9,1},{2,10},{10,2},{3,11},{11,3},{4,12},{12,4},... | collective-permute-start | bytes 491528 | tf_op jit(solution)/shard_map/ppermute | solution.py:419
  140.9 5.3 %collective-permute-start.3 = (bf16[16,8,640]{2,1,0:T(8,128)(2,1)S(1)}, bf16[16,8,640]{2,1,0:T(8,128)(2,1)S(1)}, u32[]{:S(2)}, u32[]{:S(2)}) collective-permute-start(bf16[16,8,640]{2,1,0:T(8,128)(2,1)S(1)} %all_to_all.53.mine), channel_id=1, source_target_pairs={{0,8},{8,0},{1,9},{9,1},{2,10},{10,2},{3,11},{11,3},{4,12},{12,4},... | collective-permute-start | bytes 491528 | tf_op jit(solution)/shard_map/ppermute | solution.py:419

commit v5 on v4

--- a/solution.py
+++ b/solution.py
@@ -178,14 +178,15 @@
     ]
     first.start()
     copies[0].start()
-    pick, _ = slot_of_row(core_ref[0])
-    pick = pick.astype(f32).astype(bf16)
+    copies[1].start()
+    row = lax.broadcasted_iota(jnp.int32, (128, 128), 0)
+    lane = lanes_of((128, 128))
+    same = (row == lane).astype(f32).astype(bf16)
     first.wait()
-    copies[1].start()
-    rt_ref[...] = dot(pick, router[...], NT).astype(bf16)
-    grad = is_grad_row((256, TOK))
-    lane = lanes_of((256, 128))
-    stats = jnp.zeros((256, 128), f32)
+    rt_ref[...] = dot(same, router[...], NT).astype(bf16)
+    low_core = core_ref[0] == 0
+    grad = is_grad_row((128, TOK))
+    stats = jnp.zeros((128, 128), f32)
     for c in range(CLIPS):
         copies[c].wait()
         for copy in copies[2 * c + 2 : min(2 * c + 4, 6)]:
@@ -193,25 +194,42 @@
         logits = dot(rt_ref[...], tokens[c], NT)
         lt_ref[c] = logits
         peak = jnp.max(logits, axis=1, keepdims=True)
-        low = jnp.where(grad, 0.0, jnp.exp(logits - peak)).astype(bf16)
-        total = jnp.sum(low.astype(f32), axis=1, keepdims=True)
-        own_in[c] = low[:128]
-        weights_in[c] = low[128:]
+        low = jnp.exp(logits - peak).astype(bf16).astype(f32)
+        total = jnp.sum(low, axis=1, keepdims=True)
         raised = jnp.exp(logits - jnp.max(logits, axis=0, keepdims=True))
-        combine = raised * (2.0 / jnp.sum(raised, axis=0, keepdims=True))
-        combine = jnp.where(grad, combine, 0.0).astype(bf16)
-        own_out[c] = combine[:128]
-        weights_out[c] = combine[128:]
+        combine = raised * (1.0 / jnp.sum(raised, axis=0, keepdims=True))
+        low_up = pltpu.roll(low, 124, 0)
+        combine_down = pltpu.roll(combine, 4, 0)
+        own_in[c] = jnp.where(grad, 0.0, jnp.where(low_core, low, low_up)).astype(bf16)
+        weights_in[c] = jnp.where(grad, 0.0, jnp.where(low_core, low_up, low)).astype(bf16)
+        near = jnp.where(low_core, combine_down, combine)
+        own_out[c] = jnp.where(grad, near, 0.0).astype(bf16)
+        far = jnp.where(low_core, combine, combine_down)
+        weights_out[c] = jnp.where(grad, far, 0.0).astype(bf16)
         at = STAT + 8 * c
         stats = jnp.where(lane == at, peak, jnp.where(lane == at + 3, total, stats))
+    stats_up = pltpu.roll(stats, 124, 0)
+    grad_row = is_grad_row((128, 128))
     ones = jnp.where((lane >= STAT) & (lane % 8 == 3), 1.0, 0.0)
-    stats = spread_triple(jnp.where(is_grad_row((256, 128)), ones, stats))
-    own_stats[...] = stats[:128]
-    fill_parts(theirs, weights_in, weights_out, tokens, cot, stats[128:], copies[CLIPS:])
-
-
-def own_body(own_in, own_out, own_stats, tokens, cot, mine):
+    near = jnp.where(low_core, stats, stats_up)
+    far = jnp.where(low_core, stats_up, stats)
+    own_stats[...] = spread_triple(jnp.where(grad_row, ones, near))
+    far = spread_triple(jnp.where(grad_row, ones, far))
+    fill_parts(theirs, weights_in, weights_out, tokens, cot, far, copies[CLIPS:])
+
+
+def own_body(core_ref, own_in, own_out, own_stats, tokens, cot, rt_ref, lt_ref, mine, rt_out, lt_out):
     fill_parts(mine, own_in, own_out, tokens, cot, own_stats[...])
+    pick, _ = slot_of_row(core_ref[0])
+    rt_out[...] = dot(pick.astype(f32).astype(bf16), rt_ref[...]).astype(bf16)
+    low_core = core_ref[0] == 0
+    grad = is_grad_row((128, TOK))
+    for c in range(CLIPS):
+        logits = lt_ref[c]
+        low = jnp.where(grad, pltpu.roll(logits, 4, 0), logits)
+        high = jnp.where(grad, logits, pltpu.roll(logits, 124, 0))
+        lt_out[c, :128] = jnp.where(low_core, low, high)
+        lt_out[c, 128:] = jnp.where(low_core, high, low)
 
 
 def pair_body(a_ref, b_ref, out):
@@ -430,8 +448,8 @@
         slots_body,
         [
             values,
-            ((256, D), bf16),
-            ((CLIPS, 256, TOK), f32),
+            ((128, D), bf16),
+            ((CLIPS, 128, TOK), f32),
             (local, bf16),
             (local, bf16),
             own,
@@ -453,14 +471,18 @@
         nbytes=8 * 10**6,
         limit=24,
     )
-    (mine,) = call(
+    mine, rt, lt = call(
         own_body,
-        [(values[0], f32)],
+        [(values[0], f32), ((256, D), bf16), ((CLIPS, 256, TOK), f32)],
+        core,
         own_in,
         own_out,
         own_stats,
         tokens,
         cotangent,
+        rt,
+        lt,
+        smem=(0,),
         flops=10**9,
         nbytes=8 * 10**6,
         limit=24,

time: 148 us -> 148 us (level)
  no operation moved by 1% of the time
where the time goes in v5:
time: 148 us; the launch traced here: 147 us
  blocking collectives  110 us (74%)
  Pallas kernels  19.8 us (13%)
  starting transfers between devices  14.8 us (10%)
  waiting for transfers between devices  2.04 us (1%)
    all_to_all x9, blocking collectives, exchange(): return lax.all_to_all(x, axes, 0, 0, tiled=True)  110 us
    pallas_call x14, Pallas kernels, call(): pl.pallas_call(body, out_shape=[jax.ShapeDtypeStruct(s, t) for s, t in ou...  16.6 us
    ppermute x4, starting transfers between devices, to_partner(): return lax.ppermute(x, 'core', [(0, 1), (1, 0)])  14.8 us
    pallas_call x2, Pallas kernels, token_clips(): pl.pallas_call(functools.partial(tokens_body, clips), out_shape=jax.Shape...  3.12 us
  transfers between devices with their start and end apart: 4, of which 2 were waited for; matrix products, arithmetic and copies ran while one was open for 0% of the time, Pallas kernels for 4%

profile of v5, /device:TPU:1, one launch (start us, length us, event | category | flops | bytes accessed | tf_op | source)
XLA Modules:
  0.0 147.4 jit_solution(9273178271377349283)
XLA Ops:
  0.6 5.0 %shard_map.68 = (bf16[8,16,8,512]{3,2,1,0:T(8,128)(2,1)S(1)}, bf16[128,1280]{1,0:T(8,128)(2,1)S(1)}, f32[3,128,256]{2,1,0:T(8,128)S(1)}, bf16[3,256,1280]{2,1,0:...) custom-call(s32[1]{0:T(128)} %bitcast.core_ref, ...), custom_call_target="tpu_custom_call" | custom-call | flops 3000000000 | bytes 8000000 | tf_op jit(solution)/shard_map/pallas_call | solution.py:133
  5.6 3.3 %collective-permute-start = (bf16[8,16,8,512]{3,2,1,0:T(8,128)(2,1)S(1)}, bf16[8,16,8,512]{3,2,1,0:T(8,128)(2,1)S(1)}, u32[]{:S(2)}, u32[]{:S(2)}) collective-permute-start(bf16[8,16,8,512]{3,2,1,0:T(8,128)(2,1)S(1)} %get-tuple-element.38), channel_id=1, source_target_pairs={{0,8},{8,0},{1,9},{9,1},{2,10},{10,2},{3,11},{11,3},{4,12},{12,4},... | collective-permute-start | bytes 3145736 | tf_op jit(solution)/shard_map/ppermute | solution.py:437
  8.9 1.1 shard_map.69
  10.1 1.2 collective-permute-done.b_ref
  11.2 0.8 shard_map.70
  12.0 21.4 %all_to_all.45.x_ref = bf16[16,8,8,512]{3,2,1,0:T(8,128)(2,1)S(1)} all-to-all(bf16[16,8,8,512]{3,2,1,0:T(8,128)(2,1)S(1)} %shard_map.70), channel_id=1, replica_groups=mesh['yl'=2,'z'=8,'core'=2,'yh'=2,'x'=4] {'yl','yh','x'}, dimensions={0} | all-to-all | bytes 2097152 | tf_op jit(solution)/shard_map/all_to_all | solution.py:433
  33.4 0.0 copy-start
  33.4 0.0 copy-start.1
  33.5 1.0 shard_map.71
  34.4 16.2 %all_to_all.46.x_ref = f32[8,8,512]{2,1,0:T(8,128)S(1)} all-to-all(f32[8,8,512]{2,1,0:T(8,128)S(1)} %shard_map.71), channel_id=1, replica_groups=mesh['yl'=2,'z'=8,'core'=2,'yh'=2,'x'=4] {'z'}, dimensions={0} | all-to-all | bytes 262144 | tf_op jit(solution)/shard_map/all_to_all | solution.py:433
  50.6 0.4 shard_map.72
  51.0 9.1 %all_to_all.47.x_ref = bf16[8,8,512]{2,1,0:T(8,128)(2,1)S(1)} all-to-all(bf16[8,8,512]{2,1,0:T(8,128)(2,1)S(1)} %get-tuple-element.39), channel_id=1, replica_groups=mesh['yl'=2,'z'=8,'core'=2,'yh'=2,'x'=4] {'yh','x'}, dimensions={0} | all-to-all | bytes 131072 | tf_op jit(solution)/shard_map/all_to_all | solution.py:433
  60.1 0.0 copy-done
  60.1 0.0 copy-done.1
  60.1 3.1 %shard_map.73 = (f32[8,8,512]{2,1,0:T(8,128)S(1)}, f32[8,128]{1,0:T(8,128)S(1)}) custom-call(bf16[8,8,512]{2,1,0:T(8,128)(2,1)S(1)} %all_to_all.47.x_ref, bf16[2,1280,640]{2,1,0:T(8,128)(2,1)S(1)} %copy-done, bf16[2,640,1280]{2,1,0:T(8,128)(2,1)S(1)} %copy-done.1), custom_call_target="tpu_custom_call" | custom-call | flops 1000000000 | bytes 8000000 | tf_op jit(solution)/shard_map/pallas_call | solution.py:133
  63.2 9.3 %all_to_all.48.x_ref = f32[8,8,512]{2,1,0:T(8,128)S(1)} all-to-all(f32[8,8,512]{2,1,0:T(8,128)S(1)} %get-tuple-element.40), channel_id=1, replica_groups=mesh['yl'=2,'z'=8,'core'=2,'yh'=2,'x'=4] {'yh','x'}, dimensions={0} | all-to-all | bytes 262144 | tf_op jit(solution)/shard_map/all_to_all | solution.py:433
  72.5 0.2 shard_map.74
  72.7 9.6 %all_to_all.49.x_ref = bf16[8,8,512]{2,1,0:T(8,128)(2,1)S(1)} all-to-all(bf16[8,8,512]{2,1,0:T(8,128)(2,1)S(1)} %shard_map.74), channel_id=1, replica_groups=mesh['yl'=2,'z'=8,'core'=2,'yh'=2,'x'=4] {'z'}, dimensions={0} | all-to-all | bytes 131072 | tf_op jit(solution)/shard_map/all_to_all | solution.py:433
  82.3 0.1 shard_map.75
  82.3 14.8 %all_to_all.50.g = bf16[16,8,8,512]{3,2,1,0:T(8,128)(2,1)S(1)} all-to-all(bf16[16,8,8,512]{3,2,1,0:T(8,128)(2,1)S(1)} %shard_map.75), channel_id=1, replica_groups=mesh['yl'=2,'z'=8,'core'=2,'yh'=2,'x'=4] {'yl','yh','x'}, dimensions={0} | all-to-all | bytes 2097152 | tf_op jit(solution)/shard_map/all_to_all | solution.py:433
  97.1 7.5 %collective-permute-start.1 = (bf16[16,8,8,512]{3,2,1,0:T(8,128)(2,1)S(1)}, bf16[16,8,8,512]{3,2,1,0:T(8,128)(2,1)S(1)}, u32[]{:S(2)}, u32[]{:S(2)}) collective-permute-start(bf16[16,8,8,512]{3,2,1,0:T(8,128)(2,1)S(1)} %all_to_all.50.g), channel_id=1, source_target_pairs={{0,8},{8,0},{1,9},{9,1},{2,10},{10,2},{3,11},{11,3},{4,12},{12,4},... | collective-permute-start | bytes 3145736 | tf_op jit(solution)/shard_map/ppermute | solution.py:437
  104.6 1.4 shard_map.76
  106.0 0.9 collective-permute-done.1.g
  106.9 2.4 %shard_map.77 = (bf16[16,8,640]{2,1,0:T(8,128)(2,1)S(1)}, bf16[16,8,640]{2,1,0:T(8,128)(2,1)S(1)}, bf16[3,256,256]{2,1,0:T(8,128)(2,1)S(1)}, bf16[3,256,256]{2,1,0:T(8,128)(2,1)S(1)}, bf16[3,128,1280]{2,1,0:T(8,128)(2,1)S(1)}) custom-call(bf16[3,256,1280]{2,1,0:T(8,128)(2,1)S(1)} %get-tuple-element.29.tokens, ...), custom_call_target="tpu_custom_call" | custom-call | flops 3000000000 | bytes 10000000 | tf_op jit(solution)/shard_map/pallas_call | solution.py:133
  109.3 0.5 collective-permute-start.2
  109.7 1.4 shard_map.78.rest_0_
  111.1 0.0 collective-permute-done.2.b_ref
  111.2 10.2 %all_to_all.51.x_ref = bf16[16,8,640]{2,1,0:T(8,128)(2,1)S(1)} all-to-all(bf16[16,8,640]{2,1,0:T(8,128)(2,1)S(1)} %shard_map.80), channel_id=1, replica_groups=mesh['yl'=2,'z'=8,'core'=2,'yh'=2,'x'=4] {'yl','yh','x'}, dimensions={0} | all-to-all | bytes 327680 | tf_op jit(solution)/shard_map/all_to_all | solution.py:433
  121.4 9.9 %all_to_all.52.x_ref = bf16[8,8,640]{2,1,0:T(8,128)(2,1)S(1)} all-to-all(bf16[8,8,640]{2,1,0:T(8,128)(2,1)S(1)} %shard_map.81), channel_id=1, replica_groups=mesh['yl'=2,'z'=8,'core'=2,'yh'=2,'x'=4] {'z'}, dimensions={0} | all-to-all | bytes 163840 | tf_op jit(solution)/shard_map/all_to_all | solution.py:433
  131.3 9.6 %all_to_all.53.mine = bf16[16,8,640]{2,1,0:T(8,128)(2,1)S(1)} all-to-all(bf16[16,8,640]{2,1,0:T(8,128)(2,1)S(1)} %shard_map.82), channel_id=1, replica_groups=mesh['yl'=2,'z'=8,'core'=2,'yh'=2,'x'=4] {'yl','yh','x'}, dimensions={0} | all-to-all | bytes 327680 | tf_op jit(solution)/shard_map/all_to_all | solution.py:433
  140.9 3.5 %collective-permute-start.3 = (bf16[16,8,640]{2,1,0:T(8,128)(2,1)S(1)}, bf16[16,8,640]{2,1,0:T(8,128)(2,1)S(1)}, u32[]{:S(2)}, u32[]{:S(2)}) collective-permute-start(bf16[16,8,640]{2,1,0:T(8,128)(2,1)S(1)} %all_to_all.53.mine), channel_id=1, source_target_pairs={{0,8},{8,0},{1,9},{9,1},{2,10},{10,2},{3,11},{11,3},{4,12},{12,4},... | collective-permute-start | bytes 491528 | tf_op jit(solution)/shard_map/ppermute | solution.py:437
  144.4 1.7 %shard_map.79 = bf16[3,256,1280]{2,1,0:T(8,128)(2,1)} custom-call(bf16[3,256,256]{2,1,0:T(8,128)(2,1)S(1)} %get-tuple-element.47.dl_ref, bf16[3,256,256]{2,1,0:T(8,128)(2,1)S(1)} %get-tuple-element.48.w_ref, bf16[256,1280]{1,0:T(8,128)(2,1)S(1)} %get-tuple-element.49.rt_ref, ...), custom_call_target="tpu_custom_call", output_to_operand_aliasing={{}: (5, {})} | custom-call | flops 1000000000 | bytes 3000000 | tf_op jit(solution)/shard_map/pallas_call | solution.py:397
  146.2 0.0 collective-permute-done.3.theirs
  146.2 1.3 shard_map.83
  (3 shorter events, 0.1 us)
Async XLA Ops:
  5.6 5.6 %collective-permute-start = (bf16[8,16,8,512]{3,2,1,0:T(8,128)(2,1)S(1)}, bf16[8,16,8,512]{3,2,1,0:T(8,128)(2,1)S(1)}, u32[]{:S(2)}, u32[]{:S(2)}) collective-permute-start(bf16[8,16,8,512]{3,2,1,0:T(8,128)(2,1)S(1)} %get-tuple-element.38), channel_id=1, source_target_pairs={{0,8},{8,0},{1,9},{9,1},{2,10},{10,2},{3,11},{11,3},{4,12},{12,4},... | collective-permute-start | bytes 3145736 | tf_op jit(solution)/shard_map/ppermute | solution.py:437
  33.4 26.6 %copy-start = (bf16[2,1280,640]{2,1,0:T(8,128)(2,1)S(1)}, bf16[2,1280,640]{2,1,0:T(8,128)(2,1)}, u32[]{:S(2)}) copy-start(bf16[2,1280,640]{2,1,0:T(8,128)(2,1)} %w_in.1) | copy-start | bytes 9830404
  33.4 26.6 %copy-start.1 = (bf16[2,640,1280]{2,1,0:T(8,128)(2,1)S(1)}, bf16[2,640,1280]{2,1,0:T(8,128)(2,1)}, u32[]{:S(2)}) copy-start(bf16[2,640,1280]{2,1,0:T(8,128)(2,1)} %w_out.1) | copy-start | bytes 9830404
  97.1 9.8 %collective-permute-start.1 = (bf16[16,8,8,512]{3,2,1,0:T(8,128)(2,1)S(1)}, bf16[16,8,8,512]{3,2,1,0:T(8,128)(2,1)S(1)}, u32[]{:S(2)}, u32[]{:S(2)}) collective-permute-start(bf16[16,8,8,512]{3,2,1,0:T(8,128)(2,1)S(1)} %all_to_all.50.g), channel_id=1, source_target_pairs={{0,8},{8,0},{1,9},{9,1},{2,10},{10,2},{3,11},{11,3},{4,12},{12,4},... | collective-permute-start | bytes 3145736 | tf_op jit(solution)/shard_map/ppermute | solution.py:437
  109.3 1.9 %collective-permute-start.2 = (bf16[16,8,640]{2,1,0:T(8,128)(2,1)S(1)}, bf16[16,8,640]{2,1,0:T(8,128)(2,1)S(1)}, u32[]{:S(2)}, u32[]{:S(2)}) collective-permute-start(bf16[16,8,640]{2,1,0:T(8,128)(2,1)S(1)} %get-tuple-element.52), channel_id=1, source_target_pairs={{0,8},{8,0},{1,9},{9,1},{2,10},{10,2},{3,11},{11,3},{4,12},{12,4},... | collective-permute-start | bytes 491528 | tf_op jit(solution)/shard_map/ppermute | solution.py:437
  140.9 5.3 %collective-permute-start.3 = (bf16[16,8,640]{2,1,0:T(8,128)(2,1)S(1)}, bf16[16,8,640]{2,1,0:T(8,128)(2,1)S(1)}, u32[]{:S(2)}, u32[]{:S(2)}) collective-permute-start(bf16[16,8,640]{2,1,0:T(8,128)(2,1)S(1)} %all_to_all.53.mine), channel_id=1, source_target_pairs={{0,8},{8,0},{1,9},{9,1},{2,10},{10,2},{3,11},{11,3},{4,12},{12,4},... | collective-permute-start | bytes 491528 | tf_op jit(solution)/shard_map/ppermute | solution.py:437

commit v6 on v5

--- a/solution.py
+++ b/solution.py
@@ -177,8 +177,8 @@
         for c in range(CLIPS)
     ]
     first.start()
-    copies[0].start()
-    copies[1].start()
+    for copy in copies:
+        copy.start()
     row = lax.broadcasted_iota(jnp.int32, (128, 128), 0)
     lane = lanes_of((128, 128))
     same = (row == lane).astype(f32).astype(bf16)
@@ -189,8 +189,6 @@
     stats = jnp.zeros((128, 128), f32)
     for c in range(CLIPS):
         copies[c].wait()
-        for copy in copies[2 * c + 2 : min(2 * c + 4, 6)]:
-            copy.start()
         logits = dot(rt_ref[...], tokens[c], NT)
         lt_ref[c] = logits
         peak = jnp.max(logits, axis=1, keepdims=True)

time: 148 us -> 149 us (level)
  no operation moved by 1% of the time
where the time goes in v6:
time: 149 us; the launch traced here: 148 us
  blocking collectives  110 us (74%)
  Pallas kernels  20.6 us (14%)
  starting transfers between devices  14.8 us (10%)
  waiting for transfers between devices  2.04 us (1%)
    all_to_all x9, blocking collectives, exchange(): return lax.all_to_all(x, axes, 0, 0, tiled=True)  110 us
    pallas_call x14, Pallas kernels, call(): pl.pallas_call(body, out_shape=[jax.ShapeDtypeStruct(s, t) for s, t in ou...  17.4 us
    ppermute x4, starting transfers between devices, to_partner(): return lax.ppermute(x, 'core', [(0, 1), (1, 0)])  14.8 us
    pallas_call x2, Pallas kernels, token_clips(): pl.pallas_call(functools.partial(tokens_body, clips), out_shape=jax.Shape...  3.12 us
  transfers between devices with their start and end apart: 4, of which 2 were waited for; matrix products, arithmetic and copies ran while one was open for 0% of the time, Pallas kernels for 4%

profile of v6, /device:TPU:1, one launch (start us, length us, event | category | flops | bytes accessed | tf_op | source)
XLA Modules:
  0.0 148.2 jit_solution(8885023929503101130)
XLA Ops:
  0.6 5.8 %shard_map.68 = (bf16[8,16,8,512]{3,2,1,0:T(8,128)(2,1)S(1)}, bf16[128,1280]{1,0:T(8,128)(2,1)S(1)}, f32[3,128,256]{2,1,0:T(8,128)S(1)}, bf16[3,256,1280]{2,1,0:...) custom-call(s32[1]{0:T(128)} %bitcast.core_ref, ...), custom_call_target="tpu_custom_call" | custom-call | flops 3000000000 | bytes 8000000 | tf_op jit(solution)/shard_map/pallas_call | solution.py:133
  6.4 3.3 %collective-permute-start = (bf16[8,16,8,512]{3,2,1,0:T(8,128)(2,1)S(1)}, bf16[8,16,8,512]{3,2,1,0:T(8,128)(2,1)S(1)}, u32[]{:S(2)}, u32[]{:S(2)}) collective-permute-start(bf16[8,16,8,512]{3,2,1,0:T(8,128)(2,1)S(1)} %get-tuple-element.38), channel_id=1, source_target_pairs={{0,8},{8,0},{1,9},{9,1},{2,10},{10,2},{3,11},{11,3},{4,12},{12,4},... | collective-permute-start | bytes 3145736 | tf_op jit(solution)/shard_map/ppermute | solution.py:435
  9.7 1.1 shard_map.69
  10.9 1.2 collective-permute-done.b_ref
  12.0 0.8 shard_map.70
  12.8 21.4 %all_to_all.45.x_ref = bf16[16,8,8,512]{3,2,1,0:T(8,128)(2,1)S(1)} all-to-all(bf16[16,8,8,512]{3,2,1,0:T(8,128)(2,1)S(1)} %shard_map.70), channel_id=1, replica_groups=mesh['yl'=2,'z'=8,'core'=2,'yh'=2,'x'=4] {'yl','yh','x'}, dimensions={0} | all-to-all | bytes 2097152 | tf_op jit(solution)/shard_map/all_to_all | solution.py:431
  34.2 0.0 copy-start
  34.2 0.0 copy-start.1
  34.2 1.0 shard_map.71
  35.2 16.2 %all_to_all.46.x_ref = f32[8,8,512]{2,1,0:T(8,128)S(1)} all-to-all(f32[8,8,512]{2,1,0:T(8,128)S(1)} %shard_map.71), channel_id=1, replica_groups=mesh['yl'=2,'z'=8,'core'=2,'yh'=2,'x'=4] {'z'}, dimensions={0} | all-to-all | bytes 262144 | tf_op jit(solution)/shard_map/all_to_all | solution.py:431
  51.4 0.4 shard_map.72
  51.8 9.1 %all_to_all.47.x_ref = bf16[8,8,512]{2,1,0:T(8,128)(2,1)S(1)} all-to-all(bf16[8,8,512]{2,1,0:T(8,128)(2,1)S(1)} %get-tuple-element.39), channel_id=1, replica_groups=mesh['yl'=2,'z'=8,'core'=2,'yh'=2,'x'=4] {'yh','x'}, dimensions={0} | all-to-all | bytes 131072 | tf_op jit(solution)/shard_map/all_to_all | solution.py:431
  60.9 0.0 copy-done
  60.9 0.0 copy-done.1
  60.9 3.1 %shard_map.73 = (f32[8,8,512]{2,1,0:T(8,128)S(1)}, f32[8,128]{1,0:T(8,128)S(1)}) custom-call(bf16[8,8,512]{2,1,0:T(8,128)(2,1)S(1)} %all_to_all.47.x_ref, bf16[2,1280,640]{2,1,0:T(8,128)(2,1)S(1)} %copy-done, bf16[2,640,1280]{2,1,0:T(8,128)(2,1)S(1)} %copy-done.1), custom_call_target="tpu_custom_call" | custom-call | flops 1000000000 | bytes 8000000 | tf_op jit(solution)/shard_map/pallas_call | solution.py:133
  64.0 9.3 %all_to_all.48.x_ref = f32[8,8,512]{2,1,0:T(8,128)S(1)} all-to-all(f32[8,8,512]{2,1,0:T(8,128)S(1)} %get-tuple-element.40), channel_id=1, replica_groups=mesh['yl'=2,'z'=8,'core'=2,'yh'=2,'x'=4] {'yh','x'}, dimensions={0} | all-to-all | bytes 262144 | tf_op jit(solution)/shard_map/all_to_all | solution.py:431
  73.3 0.2 shard_map.74
  73.5 9.6 %all_to_all.49.x_ref = bf16[8,8,512]{2,1,0:T(8,128)(2,1)S(1)} all-to-all(bf16[8,8,512]{2,1,0:T(8,128)(2,1)S(1)} %shard_map.74), channel_id=1, replica_groups=mesh['yl'=2,'z'=8,'core'=2,'yh'=2,'x'=4] {'z'}, dimensions={0} | all-to-all | bytes 131072 | tf_op jit(solution)/shard_map/all_to_all | solution.py:431
  83.0 0.1 shard_map.75
  83.1 14.8 %all_to_all.50.g = bf16[16,8,8,512]{3,2,1,0:T(8,128)(2,1)S(1)} all-to-all(bf16[16,8,8,512]{3,2,1,0:T(8,128)(2,1)S(1)} %shard_map.75), channel_id=1, replica_groups=mesh['yl'=2,'z'=8,'core'=2,'yh'=2,'x'=4] {'yl','yh','x'}, dimensions={0} | all-to-all | bytes 2097152 | tf_op jit(solution)/shard_map/all_to_all | solution.py:431
  97.9 7.5 %collective-permute-start.1 = (bf16[16,8,8,512]{3,2,1,0:T(8,128)(2,1)S(1)}, bf16[16,8,8,512]{3,2,1,0:T(8,128)(2,1)S(1)}, u32[]{:S(2)}, u32[]{:S(2)}) collective-permute-start(bf16[16,8,8,512]{3,2,1,0:T(8,128)(2,1)S(1)} %all_to_all.50.g), channel_id=1, source_target_pairs={{0,8},{8,0},{1,9},{9,1},{2,10},{10,2},{3,11},{11,3},{4,12},{12,4},... | collective-permute-start | bytes 3145736 | tf_op jit(solution)/shard_map/ppermute | solution.py:435
  105.4 1.4 shard_map.76
  106.8 0.9 collective-permute-done.1.g
  107.7 2.4 %shard_map.77 = (bf16[16,8,640]{2,1,0:T(8,128)(2,1)S(1)}, bf16[16,8,640]{2,1,0:T(8,128)(2,1)S(1)}, bf16[3,256,256]{2,1,0:T(8,128)(2,1)S(1)}, bf16[3,256,256]{2,1,0:T(8,128)(2,1)S(1)}, bf16[3,128,1280]{2,1,0:T(8,128)(2,1)S(1)}) custom-call(bf16[3,256,1280]{2,1,0:T(8,128)(2,1)S(1)} %get-tuple-element.29.tokens, ...), custom_call_target="tpu_custom_call" | custom-call | flops 3000000000 | bytes 10000000 | tf_op jit(solution)/shard_map/pallas_call | solution.py:133
  110.1 0.5 collective-permute-start.2
  110.5 1.4 shard_map.78.rest_0_
  111.9 0.0 collective-permute-done.2.b_ref
  112.0 10.2 %all_to_all.51.x_ref = bf16[16,8,640]{2,1,0:T(8,128)(2,1)S(1)} all-to-all(bf16[16,8,640]{2,1,0:T(8,128)(2,1)S(1)} %shard_map.80), channel_id=1, replica_groups=mesh['yl'=2,'z'=8,'core'=2,'yh'=2,'x'=4] {'yl','yh','x'}, dimensions={0} | all-to-all | bytes 327680 | tf_op jit(solution)/shard_map/all_to_all | solution.py:431
  122.2 9.9 %all_to_all.52.x_ref = bf16[8,8,640]{2,1,0:T(8,128)(2,1)S(1)} all-to-all(bf16[8,8,640]{2,1,0:T(8,128)(2,1)S(1)} %shard_map.81), channel_id=1, replica_groups=mesh['yl'=2,'z'=8,'core'=2,'yh'=2,'x'=4] {'z'}, dimensions={0} | all-to-all | bytes 163840 | tf_op jit(solution)/shard_map/all_to_all | solution.py:431
  132.1 9.6 %all_to_all.53.mine = bf16[16,8,640]{2,1,0:T(8,128)(2,1)S(1)} all-to-all(bf16[16,8,640]{2,1,0:T(8,128)(2,1)S(1)} %shard_map.82), channel_id=1, replica_groups=mesh['yl'=2,'z'=8,'core'=2,'yh'=2,'x'=4] {'yl','yh','x'}, dimensions={0} | all-to-all | bytes 327680 | tf_op jit(solution)/shard_map/all_to_all | solution.py:431
  141.7 3.5 %collective-permute-start.3 = (bf16[16,8,640]{2,1,0:T(8,128)(2,1)S(1)}, bf16[16,8,640]{2,1,0:T(8,128)(2,1)S(1)}, u32[]{:S(2)}, u32[]{:S(2)}) collective-permute-start(bf16[16,8,640]{2,1,0:T(8,128)(2,1)S(1)} %all_to_all.53.mine), channel_id=1, source_target_pairs={{0,8},{8,0},{1,9},{9,1},{2,10},{10,2},{3,11},{11,3},{4,12},{12,4},... | collective-permute-start | bytes 491528 | tf_op jit(solution)/shard_map/ppermute | solution.py:435
  145.2 1.7 %shard_map.79 = bf16[3,256,1280]{2,1,0:T(8,128)(2,1)} custom-call(bf16[3,256,256]{2,1,0:T(8,128)(2,1)S(1)} %get-tuple-element.47.dl_ref, bf16[3,256,256]{2,1,0:T(8,128)(2,1)S(1)} %get-tuple-element.48.w_ref, bf16[256,1280]{1,0:T(8,128)(2,1)S(1)} %get-tuple-element.49.rt_ref, ...), custom_call_target="tpu_custom_call", output_to_operand_aliasing={{}: (5, {})} | custom-call | flops 1000000000 | bytes 3000000 | tf_op jit(solution)/shard_map/pallas_call | solution.py:395
  147.0 0.0 collective-permute-done.3.theirs
  147.0 1.3 shard_map.83
  (3 shorter events, 0.1 us)
Async XLA Ops:
  6.4 5.6 %collective-permute-start = (bf16[8,16,8,512]{3,2,1,0:T(8,128)(2,1)S(1)}, bf16[8,16,8,512]{3,2,1,0:T(8,128)(2,1)S(1)}, u32[]{:S(2)}, u32[]{:S(2)}) collective-permute-start(bf16[8,16,8,512]{3,2,1,0:T(8,128)(2,1)S(1)} %get-tuple-element.38), channel_id=1, source_target_pairs={{0,8},{8,0},{1,9},{9,1},{2,10},{10,2},{3,11},{11,3},{4,12},{12,4},... | collective-permute-start | bytes 3145736 | tf_op jit(solution)/shard_map/ppermute | solution.py:435
  34.2 26.6 %copy-start = (bf16[2,1280,640]{2,1,0:T(8,128)(2,1)S(1)}, bf16[2,1280,640]{2,1,0:T(8,128)(2,1)}, u32[]{:S(2)}) copy-start(bf16[2,1280,640]{2,1,0:T(8,128)(2,1)} %w_in.1) | copy-start | bytes 9830404
  34.2 26.6 %copy-start.1 = (bf16[2,640,1280]{2,1,0:T(8,128)(2,1)S(1)}, bf16[2,640,1280]{2,1,0:T(8,128)(2,1)}, u32[]{:S(2)}) copy-start(bf16[2,640,1280]{2,1,0:T(8,128)(2,1)} %w_out.1) | copy-start | bytes 9830404
  97.9 9.8 %collective-permute-start.1 = (bf16[16,8,8,512]{3,2,1,0:T(8,128)(2,1)S(1)}, bf16[16,8,8,512]{3,2,1,0:T(8,128)(2,1)S(1)}, u32[]{:S(2)}, u32[]{:S(2)}) collective-permute-start(bf16[16,8,8,512]{3,2,1,0:T(8,128)(2,1)S(1)} %all_to_all.50.g), channel_id=1, source_target_pairs={{0,8},{8,0},{1,9},{9,1},{2,10},{10,2},{3,11},{11,3},{4,12},{12,4},... | collective-permute-start | bytes 3145736 | tf_op jit(solution)/shard_map/ppermute | solution.py:435
  110.1 1.9 %collective-permute-start.2 = (bf16[16,8,640]{2,1,0:T(8,128)(2,1)S(1)}, bf16[16,8,640]{2,1,0:T(8,128)(2,1)S(1)}, u32[]{:S(2)}, u32[]{:S(2)}) collective-permute-start(bf16[16,8,640]{2,1,0:T(8,128)(2,1)S(1)} %get-tuple-element.52), channel_id=1, source_target_pairs={{0,8},{8,0},{1,9},{9,1},{2,10},{10,2},{3,11},{11,3},{4,12},{12,4},... | collective-permute-start | bytes 491528 | tf_op jit(solution)/shard_map/ppermute | solution.py:435
  141.7 5.3 %collective-permute-start.3 = (bf16[16,8,640]{2,1,0:T(8,128)(2,1)S(1)}, bf16[16,8,640]{2,1,0:T(8,128)(2,1)S(1)}, u32[]{:S(2)}, u32[]{:S(2)}) collective-permute-start(bf16[16,8,640]{2,1,0:T(8,128)(2,1)S(1)} %all_to_all.53.mine), channel_id=1, source_target_pairs={{0,8},{8,0},{1,9},{9,1},{2,10},{10,2},{3,11},{11,3},{4,12},{12,4},... | collective-permute-start | bytes 491528 | tf_op jit(solution)/shard_map/ppermute | solution.py:435
